TPU v7x, 1024 devices: a whole 4x8x16 slice. The times are simulated.
1024 devices in a mesh: dp: 16 (over z), node: 4 (over x), local: 16 (over y, core).
Axes of the slice: x: 4, y: 8, z: 16, core: 2. Of those that a mesh axis runs over, the one named last changes fastest.
Arguments:
- tokens: bfloat16 [16384, 7168], P(('dp', 'node'), 'local'), parts along dimension 0, may hold values from -6 to 6
- routes: int32 [16384, 2], P(('dp', 'node')), parts along dimension 0, may hold values from 0 to 3, all different within a row; in each aligned block of 256 rows (0 to 255, 256 to 511, ...) at most 160 rows name the same one
- route_weight: float32 [16384, 2], P(('dp', 'node')), parts along dimension 0, may hold values from 0.1 to 1
- w_gate: bfloat16 [4, 7168, 2048], P('node', None, 'local'), may hold values from -0.0625 to 0.0625
- w_up: bfloat16 [4, 7168, 2048], P('node', None, 'local'), may hold values from -0.0625 to 0.0625
- w_down: bfloat16 [4, 2048, 7168], P('node', None, 'local'), may hold values from -0.125 to 0.125
Outputs:
- mixed: bfloat16 [16384, 7168], P(('dp', 'node'), 'local'), parts along dimension 0
There are 16 independent parts, one for each index of `dp`. A program takes and returns all parts, laid end to end along the dimension named above; an argument that names none is the same for every part. Nothing has to cross between parts.
Inputs may be any that keep to these rules, and one draw needn't show every extreme that they name: `routes`: each token names 2 different experts. Among the 256 tokens of one index of node (aligned blocks of rows) no expert is named more than 160 times, a bound that some block reaches.
All inputs are finite; a program needn't handle non-finite values.
Results may differ from a plain program's by a relative error of at most 0.0057.
Values may be sent and summed in bfloat16 or wider, within the bound.
No kernel may reach another device: no remote copies, remote signals or barrier semaphores. Data moves between devices by JAX's collectives and lax.ppermute only.
A program may use at most 64 MiB of HBM per device.

v0:
```python
import functools

import jax
import jax.numpy as jnp
from jax import lax
from jax.experimental import pallas as pl
from jax.experimental.pallas import tpu as pltpu
from jax.sharding import Mesh, PartitionSpec as P

F32, BF16 = jnp.float32, jnp.bfloat16
SWAP = [(0, 1), (1, 0)]
VMEM_LIMIT = 52 * 1024 * 1024
LAST_LIMIT = 32 * 1024 * 1024
NT = (((1,), (1,)), ((), ()))
TN = (((0,), (0,)), ((), ()))


def whole(shape):
    return pl.BlockSpec(shape, lambda i: (0,) * len(shape))


def dispatch_kernel(core_ref, own_ref, other_ref, routes_ref, rows_ref, pick_ref, both):
    width, count = own_ref.shape
    nodes, half, _ = rows_ref.shape
    core = core_ref[0]
    both[pl.ds(pl.multiple_of(core * width, width), width), :] = own_ref[...]
    both[pl.ds(pl.multiple_of((1 - core) * width, width), width), :] = other_ref[...]
    first, second = routes_ref[0:1, :], routes_ref[1:2, :]
    experts = lax.broadcasted_iota(jnp.int32, (8, count), 0)
    member = (first == experts) | (second == experts)
    before = lax.broadcasted_iota(jnp.int32, (count, count), 0)
    after = lax.broadcasted_iota(jnp.int32, (count, count), 1)
    slots = jnp.dot(
        member.astype(F32).astype(BF16),
        (before < after).astype(F32).astype(BF16),
        preferred_element_type=F32,
    ).astype(jnp.int32)
    for k, route in enumerate((first, second)):
        slot = jnp.sum(jnp.where(route == experts, slots, 0), axis=0, keepdims=True)
        pick_ref[k : k + 1, :] = route * (2 * half) + slot
    wanted = lax.broadcasted_iota(jnp.int32, (half, count), 0) + core * half
    for e in range(nodes):
        chosen = (first == e) | (second == e)
        place = jnp.where(chosen, slots[e : e + 1, :], -1)
        picker = (wanted == place).astype(F32).astype(BF16)
        rows_ref[e] = lax.dot_general(picker, both[...], NT, preferred_element_type=F32).astype(BF16)


def dispatch(core, own, other, routes, nodes, half):
    width, count = own.shape
    return pl.pallas_call(
        dispatch_kernel,
        out_shape=(
            jax.ShapeDtypeStruct((nodes, half, 2 * width), BF16),
            jax.ShapeDtypeStruct((2, count), jnp.int32),
        ),
        grid=(1,),
        in_specs=[pl.BlockSpec(memory_space=pltpu.SMEM)] + [whole(x.shape) for x in (own, other, routes)],
        out_specs=(whole((nodes, half, 2 * width)), whole((2, count))),
        scratch_shapes=[pltpu.VMEM((2 * width, count), BF16)],
        compiler_params=pltpu.CompilerParams(vmem_limit_bytes=VMEM_LIMIT),
        cost_estimate=pl.CostEstimate(flops=2 * nodes * half * count * 2 * width, bytes_accessed=2000000, transcendentals=0),
    )(core, own, other, routes)


def gate_up_kernel(layout, rest, last, idx_ref, *refs):
    refs = list(refs)
    x = []
    for parts in layout:
        x.append(jnp.concatenate([refs.pop(0)[...] for _ in range(parts)], axis=0))
    w = []
    for _ in layout:
        w.append(jnp.concatenate([refs.pop(0)[...] for _ in range(4)], axis=1))
    total = jnp.dot(jnp.concatenate(x, axis=1), jnp.concatenate(w, axis=0), preferred_element_type=F32)
    if rest:
        total = total + refs.pop(0)[...]
    out = refs.pop(0)
    if not last:
        out[...] = total
        return
    core = idx_ref[idx_ref.shape[0] - 1]
    hid = total.shape[1] // 4
    gate, up = total[:, :hid], total[:, hid : 2 * hid]
    own = gate / (1.0 + jnp.exp(-gate)) * up
    gate, up = total[:, 2 * hid : 3 * hid], total[:, 3 * hid :]
    other = gate / (1.0 + jnp.exp(-gate)) * up
    left = jnp.where(core == 0, own, other).astype(BF16)
    right = jnp.where(core == 0, other, own).astype(BF16)
    for k in range(out.shape[0]):
        out[k, :, :hid] = left
        out[k, :, hid:] = right


def gate_up(items, sums, weights, idx, last=None):
    operands = [b for blocks, _ in items for b in blocks]
    rows = sum(b.shape[0] for b in items[0][0])
    width, hid = operands[0].shape[1], weights[0].shape[1]
    full = lambda shape: pl.BlockSpec(shape, lambda i, idx: (0,) * len(shape))
    in_specs = [full(b.shape) for b in operands]
    for _, at in items:
        for w in weights:
            in_specs.append(pl.BlockSpec((width, hid), functools.partial(lambda at, i, idx: (idx[at], 0), at)))
            operands.append(w)
    aliases = {}
    if sums is not None:
        if last is None:
            aliases[1 + len(operands)] = 0
        in_specs.append(full(sums.shape))
        operands.append(sums)
    shape = jax.ShapeDtypeStruct((rows, 4 * hid), F32)
    if last is not None:
        shape = jax.ShapeDtypeStruct((last, rows, 2 * hid), BF16)
    return pl.pallas_call(
        functools.partial(
            gate_up_kernel, tuple(len(blocks) for blocks, _ in items), sums is not None, last is not None
        ),
        grid_spec=pltpu.PrefetchScalarGridSpec(
            num_scalar_prefetch=1, grid=(1,), in_specs=in_specs, out_specs=full(shape.shape)
        ),
        out_shape=shape,
        input_output_aliases=aliases,
        compiler_params=pltpu.CompilerParams(vmem_limit_bytes=VMEM_LIMIT if last is None else LAST_LIMIT),
        cost_estimate=pl.CostEstimate(
            flops=8 * len(items) * rows * width * hid,
            bytes_accessed=len(items) * width * (8 * hid + 2 * rows) + 16 * rows * hid,
            transcendentals=0,
        ),
    )(idx, *operands)


def down_kernel(core_ref, hidden_ref, own_ref, other_ref, out_ref, total):
    k = pl.program_id(0)
    hidden = jnp.concatenate([hidden_ref[j] for j in range(hidden_ref.shape[0])], axis=1)
    w = jnp.concatenate([own_ref[...], other_ref[...]], axis=0)
    part = lax.dot_general(hidden, w, NT, preferred_element_type=F32)

    @pl.when(k == 0)
    def _():
        total[...] = part

    @pl.when(k > 0)
    def _():
        nodes, _, half, width = out_ref.shape
        core = core_ref[0]
        for side, at in ((core, 0), (1 - core, width)):
            for e in range(nodes):
                rows, cols = slice(e * half, (e + 1) * half), slice(at, at + width)
                out_ref[e, side] = (total[rows, cols] + part[rows, cols]).astype(BF16)


def down(core, hidden, own, other, half):
    chips, rows, depth = hidden.shape
    width = own.shape[0]
    nodes = rows // half
    step = chips // 2
    return pl.pallas_call(
        down_kernel,
        grid=(2,),
        out_shape=jax.ShapeDtypeStruct((nodes, 2, half, width), BF16),
        in_specs=[
            pl.BlockSpec(memory_space=pltpu.SMEM),
            pl.BlockSpec((step, rows, depth), lambda k: (k, 0, 0)),
            pl.BlockSpec((width, step * depth), lambda k: (0, k)),
            pl.BlockSpec((width, step * depth), lambda k: (0, k)),
        ],
        out_specs=pl.BlockSpec((nodes, 2, half, width), lambda k: (0, 0, 0, 0)),
        scratch_shapes=[pltpu.VMEM((rows, 2 * width), F32)],
        compiler_params=pltpu.CompilerParams(vmem_limit_bytes=VMEM_LIMIT),
        cost_estimate=pl.CostEstimate(flops=4 * rows * depth * chips * width, bytes_accessed=6000000, transcendentals=0),
    )(core, hidden, own, other)


def combine_kernel(rows_ref, pick_ref, weight_ref, out_ref):
    total = rows_ref.shape[0]
    count = pick_ref.shape[1]
    row = lax.broadcasted_iota(jnp.int32, (total, count), 0)
    scale = jnp.zeros((total, count), F32)
    for k in range(pick_ref.shape[0]):
        scale = jnp.where(row == pick_ref[k : k + 1, :], weight_ref[k : k + 1, :], scale)
    high = scale.astype(BF16)
    low = (scale - high.astype(F32)).astype(BF16)
    rows = rows_ref[...]
    mixed = lax.dot_general(rows, high, TN, preferred_element_type=F32)
    mixed = mixed + lax.dot_general(rows, low, TN, preferred_element_type=F32)
    out_ref[...] = mixed.astype(BF16)


def combine(rows, pick, weight):
    total, width = rows.shape
    count = pick.shape[1]
    return pl.pallas_call(
        combine_kernel,
        out_shape=jax.ShapeDtypeStruct((width, count), BF16),
        grid=(1,),
        in_specs=[whole(x.shape) for x in (rows, pick, weight)],
        out_specs=whole((width, count)),
        compiler_params=pltpu.CompilerParams(vmem_limit_bytes=VMEM_LIMIT),
        cost_estimate=pl.CostEstimate(flops=4 * total * count * width, bytes_accessed=1500000, transcendentals=0),
    )(rows, pick, weight)


def local(tokens, routes, route_weight, w_gate, w_up, w_down):
    nodes, chips = lax.axis_size("node"), lax.axis_size("y")
    count, width = tokens.shape
    capacity = min(count, 5 * count * routes.shape[1] // (4 * nodes))
    half = capacity // 2
    core, here = lax.axis_index("core").astype(jnp.int32)[None], lax.axis_index("y")
    idx = jnp.concatenate([lax.rem(here + jnp.arange(chips), chips).astype(jnp.int32), core])

    def hop(x, distance):
        return lax.ppermute(x, "y", [(i, (i + distance) % chips) for i in range(chips)])

    def across(x):
        return lax.ppermute(x, "core", SWAP)

    def exchange(x, axes):
        return lax.all_to_all(x, axes, split_axis=0, concat_axis=0, tiled=True)

    own = tokens.T
    rows, pick = dispatch(core, own, across(own), routes.T, nodes, half)
    size = nodes * half
    gate_w, up_w, rows = lax.optimization_barrier((w_gate[0], w_up[0], rows))
    rows = exchange(rows, "node").reshape(size, 2 * width)
    weights = (gate_w, up_w, across(gate_w), across(up_w))

    up_y, down_y = hop(rows, 1), hop(rows, -1)
    sums = gate_up([((rows,), 0), ((up_y,), chips - 1), ((down_y,), 1)], None, weights, idx)
    for s in range(2, chips // 2):
        up_y, down_y = hop(up_y, 1), hop(down_y, -1)
        new = gate_up([((up_y,), chips - s), ((down_y,), s)], sums, weights, idx)
        down_y, sums = lax.optimization_barrier((down_y, sums))
        sums = new
    pairs = [(y, side) for y in range(chips) for side in range(2)]
    pairs = [(2 * y + side, 2 * ((y + 1 - 2 * side) % chips) + side) for y, side in pairs]
    far = lax.ppermute(jnp.where(core[0] == 0, up_y, down_y), ("y", "core"), pairs)
    hidden = gate_up([((far,), chips // 2)], sums, weights, idx, last=chips)
    hidden, down_w = lax.optimization_barrier((hidden, w_down[0].T))
    hidden, down_other = exchange(hidden, "y"), across(down_w)
    out = down(core, hidden, down_w, down_other, half)
    back = exchange(out.reshape(2 * nodes, half, width), ("node", "core"))
    return combine(back.reshape(2 * nodes * half, width), pick, route_weight.T).T


def solution(mesh):
    shape = mesh.devices.shape
    split = Mesh(mesh.devices.reshape(shape[:2] + (shape[2] // 2, 2)), ("dp", "node", "y", "core"))
    rows, cols = ("dp", "node"), ("y", "core")
    return jax.shard_map(
        local,
        mesh=split,
        in_specs=(
            P(rows, cols),
            P(rows, None),
            P(rows, None),
            P("node", None, cols),
            P("node", None, cols),
            P("node", None, cols),
        ),
        out_specs=P(rows, cols),
        check_vma=False,
    )
```

profile of v0, /device:TPU:1, one launch (start us, length us, event | category | flops | bytes accessed | tf_op | source)
XLA Modules:
  0.0 155.9 jit_solution(8729471927751116451)
XLA Ops:
  0.0 16.1 %collective-permute-start = (bf16[448,256]{1,0:T(8,128)(2,1)}, bf16[448,256]{1,0:T(8,128)(2,1)S(1)}, u32[]{:S(2)}, u32[]{:S(2)}) collective-permute-start(bf16[448,256]{1,0:T(8,128)(2,1)} %bitcast.36), channel_id=1, source_target_pairs={{0,1},{1,0},{2,3},{3,2},{4,5},{5,4},{6,7},{7,6},{8,9},{9,8},{10,11... | collective-permute-start | bytes 688136 | tf_op jit(solution)/shard_map/ppermute | solution.py:214
  16.1 1.3 collective-permute-done.other_ref
  17.4 0.0 copy-start.7
  17.4 0.9 copy-done.7
  18.3 0.0 copy-start.8
  18.3 0.7 copy-done.8
  19.0 0.8 shard_map.64
  19.7 0.0 copy-start.10
  19.7 2.3 %collective-permute-start.6 = (bf16[7168,128]{1,0:T(8,128)(2,1)}, bf16[7168,128]{1,0:T(8,128)(2,1)S(1)}, u32[]{:S(2)}, u32[]{:S(2)}) collective-permute-start(bf16[7168,128]{1,0:T(8,128)(2,1)} %bitcast.13), channel_id=1, source_target_pairs={{0,1},{1,0},{2,3},{3,2},{4,5},{5,4},{6,7},{7,6},{8,9},{9,8},{10,11... | collective-permute-start | bytes 5505032 | tf_op jit(solution)/shard_map/ppermute | solution.py:214
  22.0 2.0 %collective-permute-start.7 = (bf16[7168,128]{1,0:T(8,128)(2,1)}, bf16[7168,128]{1,0:T(8,128)(2,1)}, u32[]{:S(2)}, u32[]{:S(2)}) collective-permute-start(bf16[7168,128]{1,0:T(8,128)(2,1)} %bitcast.22), channel_id=1, source_target_pairs={{0,1},{1,0},{2,3},{3,2},{4,5},{5,4},{6,7},{7,6},{8,9},{9,8},{10,11... | collective-permute-start | bytes 5505032 | tf_op jit(solution)/shard_map/ppermute | solution.py:214
  24.1 11.8 %all_to_all.15 = bf16[4,80,896]{2,1,0:T(8,128)(2,1)S(1)} all-to-all(bf16[4,80,896]{2,1,0:T(8,128)(2,1)S(1)} %get-tuple-element.15), channel_id=1, replica_groups=mesh['dp'=16,'node'=4,'y'=8,'core'=2] {'node'}, dimensions={0} | all-to-all | bytes 1146880 | tf_op jit(solution)/shard_map/all_to_all | solution.py:217
  35.9 1.9 %collective-permute-start.4 = (bf16[320,896]{1,0:T(8,128)(2,1)S(1)}, bf16[320,896]{1,0:T(8,128)(2,1)}, u32[]{:S(2)}, u32[]{:S(2)}) collective-permute-start(bf16[320,896]{1,0:T(8,128)(2,1)S(1)} %bitcast.32), channel_id=1, source_target_pairs={{0,14},{2,0},{4,2},{6,4},{8,6},{10,8},{12,10},{14,12},{1,15},{3,1}... | collective-permute-start | bytes 1720328 | tf_op jit(solution)/shard_map/ppermute | solution.py:211
  37.9 3.4 %collective-permute-start.1 = (bf16[320,896]{1,0:T(8,128)(2,1)S(1)}, bf16[320,896]{1,0:T(8,128)(2,1)}, u32[]{:S(2)}, u32[]{:S(2)}) collective-permute-start(bf16[320,896]{1,0:T(8,128)(2,1)S(1)} %bitcast.33), channel_id=1, source_target_pairs={{0,2},{2,4},{4,6},{6,8},{8,10},{10,12},{12,14},{14,0},{1,3},{3,5},... | collective-permute-start | bytes 1720328 | tf_op jit(solution)/shard_map/ppermute | solution.py:211
  41.2 9.7 %collective-permute-done.4.refs_2_ = bf16[320,896]{1,0:T(8,128)(2,1)} collective-permute-done((bf16[320,896]{1,0:T(8,128)(2,1)S(1)}, bf16[320,896]{1,0:T(8,128)(2,1)}, u32[]{:S(2)}, u32[]{:S(2)}) %collective-permute-start.4) | collective-permute-done | bytes 573472 | tf_op jit(solution)/shard_map/ppermute | solution.py:211
  50.9 3.4 %collective-permute-start.5 = (bf16[320,896]{1,0:T(8,128)(2,1)}, bf16[320,896]{1,0:T(8,128)(2,1)S(1)}, u32[]{:S(2)}, u32[]{:S(2)}) collective-permute-start(bf16[320,896]{1,0:T(8,128)(2,1)} %collective-permute-done.4.refs_2_), channel_id=1, source_target_pairs={{0,14},{2,0},{4,2},{6,4},{8,6},{10,8},{12,10},{14,12},{1,15},{3,1}... | collective-permute-start | bytes 1720328 | tf_op jit(solution)/shard_map/ppermute | solution.py:211
  54.3 0.0 collective-permute-done.1.refs_1_
  54.3 0.0 copy-done.10
  54.3 1.9 %collective-permute-start.2 = (bf16[320,896]{1,0:T(8,128)(2,1)}, bf16[320,896]{1,0:T(8,128)(2,1)S(1)}, u32[]{:S(2)}, u32[]{:S(2)}) collective-permute-start(bf16[320,896]{1,0:T(8,128)(2,1)} %collective-permute-done.1.refs_1_), channel_id=1, source_target_pairs={{0,2},{2,4},{4,6},{6,8},{8,10},{10,12},{12,14},{14,0},{1,3},{3,5},... | collective-permute-start | bytes 1720328 | tf_op jit(solution)/shard_map/ppermute | solution.py:211
  56.3 0.1 pad_add_fusion.idx_ref
  56.4 0.0 collective-permute-done.6.refs_5_.refs_9_.refs_13_.refs_4_.refs_8_.refs_3_
  56.4 0.0 copy-start.2
  56.4 0.0 collective-permute-done.7.refs_6_.refs_10_.refs_14_.refs_5_.refs_9_.refs_4_
  56.4 1.2 copy-done.2
  57.6 4.5 %shard_map.65.refs_10_ = f32[320,512]{1,0:T(8,128)} custom-call(s32[9]{0:T(128)S(1)} %pad_add_fusion.idx_ref, bf16[320,896]{1,0:T(8,128)(2,1)S(1)} %bitcast.34, bf16[320,896]{1,0:T(8,128)(2,1)} %collective-permute-done.1.refs_1_, bf16[320,896]{1,0:T(8,128)(2,1)} %collective-permute-done.4.refs_2_, bf16[7168,128]{1,0:T(8,128)(2,1)} %bitcast.14, ...), custom_call_target="tpu_custom_call" | custom-call | flops 880803840 | bytes 5128192 | tf_op jit(solution)/shard_map/pallas_call | solution.py:113
  62.1 0.0 copy-start.5
  62.1 0.5 copy-done.5
  62.6 2.4 %collective-permute-done.5.refs_1_ = bf16[320,896]{1,0:T(8,128)(2,1)S(1)} collective-permute-done((bf16[320,896]{1,0:T(8,128)(2,1)}, bf16[320,896]{1,0:T(8,128)(2,1)S(1)}, u32[]{:S(2)}, u32[]{:S(2)}) %collective-permute-start.5) | collective-permute-done | bytes 573472 | tf_op jit(solution)/shard_map/ppermute | solution.py:211
  65.1 4.9 %collective-permute-start.8 = (bf16[320,896]{1,0:T(8,128)(2,1)S(1)}, bf16[320,896]{1,0:T(8,128)(2,1)S(1)}, u32[]{:S(2)}, u32[]{:S(2)}) collective-permute-start(bf16[320,896]{1,0:T(8,128)(2,1)S(1)} %collective-permute-done.5.refs_1_), channel_id=1, source_target_pairs={{0,14},{2,0},{4,2},{6,4},{8,6},{10,8},{12,10},{14,12},{1,15},{3,1}... | collective-permute-start | bytes 1720328 | tf_op jit(solution)/shard_map/ppermute | solution.py:211
  70.0 0.0 collective-permute-done.2.refs_0_
  70.0 1.9 %collective-permute-start.3 = (bf16[320,896]{1,0:T(8,128)(2,1)S(1)}, bf16[320,896]{1,0:T(8,128)(2,1)S(1)}, u32[]{:S(2)}, u32[]{:S(2)}) collective-permute-start(bf16[320,896]{1,0:T(8,128)(2,1)S(1)} %collective-permute-done.2.refs_0_), channel_id=1, source_target_pairs={{0,2},{2,4},{4,6},{6,8},{8,10},{10,12},{12,14},{14,0},{1,3},{3,5},... | collective-permute-start | bytes 1720328 | tf_op jit(solution)/shard_map/ppermute | solution.py:211
  71.9 0.0 copy-start.4
  71.9 1.1 copy-done.4
  73.0 0.0 copy-start.6
  73.0 0.6 copy-done.6
  73.6 2.9 %shard_map.66.refs_10_ = f32[320,512]{1,0:T(8,128)S(1)} custom-call(s32[9]{0:T(128)S(1)} %copy-done.6, bf16[320,896]{1,0:T(8,128)(2,1)S(1)} %collective-permute-done.2.refs_0_, bf16[320,896]{1,0:T(8,128)(2,1)S(1)} %collective-permute-done.5.refs_1_, bf16[7168,128]{1,0:T(8,128)(2,1)} %bitcast.17, ...), custom_call_target="tpu_custom_call", output_to_operand_aliasing={{}: (11, {})} | custom-call | flops 587202560 | bytes 3637248 | tf_op jit(solution)/shard_map/pallas_call | solution.py:113
  76.5 2.7 %collective-permute-done.8.refs_1_ = bf16[320,896]{1,0:T(8,128)(2,1)S(1)} collective-permute-done((bf16[320,896]{1,0:T(8,128)(2,1)S(1)}, bf16[320,896]{1,0:T(8,128)(2,1)S(1)}, u32[]{:S(2)}, u32[]{:S(2)}) %collective-permute-start.8) | collective-permute-done | bytes 573472 | tf_op jit(solution)/shard_map/ppermute | solution.py:211
  79.1 5.1 %collective-permute-done.3.refs_0_ = bf16[320,896]{1,0:T(8,128)(2,1)S(1)} collective-permute-done((bf16[320,896]{1,0:T(8,128)(2,1)S(1)}, bf16[320,896]{1,0:T(8,128)(2,1)S(1)}, u32[]{:S(2)}, u32[]{:S(2)}) %collective-permute-start.3) | collective-permute-done | bytes 573472 | tf_op jit(solution)/shard_map/ppermute | solution.py:211
  84.2 0.1 broadcast_select_fusion
  84.3 0.0 copy-start
  84.3 0.0 copy-start.1
  84.3 0.0 copy-start.3
  84.3 2.3 %collective-permute-start.9 = (bf16[320,896]{1,0:T(8,128)(2,1)S(1)}, bf16[320,896]{1,0:T(8,128)(2,1)S(1)}, u32[]{:S(2)}, u32[]{:S(2)}) collective-permute-start(bf16[320,896]{1,0:T(8,128)(2,1)S(1)} %broadcast_select_fusion), channel_id=1, source_target_pairs={{0,2},{1,15},{2,4},{3,1},{4,6},{5,3},{6,8},{7,5},{8,10},{9,7},{10,... | collective-permute-start | bytes 1720328 | tf_op jit(solution)/shard_map/ppermute | solution.py:235
  86.6 2.9 %shard_map.67.refs_5_ = f32[320,512]{1,0:T(8,128)S(1)} custom-call(s32[9]{0:T(128)S(1)} %copy-done.6, bf16[320,896]{1,0:T(8,128)(2,1)S(1)} %collective-permute-done.3.refs_0_, bf16[320,896]{1,0:T(8,128)(2,1)S(1)} %collective-permute-done.8.refs_1_, bf16[7168,128]{1,0:T(8,128)(2,1)} %bitcast.19, ...), custom_call_target="tpu_custom_call", output_to_operand_aliasing={{}: (11, {})} | custom-call | flops 587202560 | bytes 3637248 | tf_op jit(solution)/shard_map/pallas_call | solution.py:113
  89.5 5.8 %collective-permute-done.9.refs_0_ = bf16[320,896]{1,0:T(8,128)(2,1)S(1)} collective-permute-done((bf16[320,896]{1,0:T(8,128)(2,1)S(1)}, bf16[320,896]{1,0:T(8,128)(2,1)S(1)}, u32[]{:S(2)}, u32[]{:S(2)}) %collective-permute-start.9) | collective-permute-done | bytes 573472 | tf_op jit(solution)/shard_map/ppermute | solution.py:235
  95.3 0.0 copy-done
  95.3 0.0 copy-done.1
  95.3 0.0 copy-done.3
  95.3 3.2 %shard_map.68 = bf16[8,320,256]{2,1,0:T(8,128)(2,1)} custom-call(s32[9]{0:T(128)S(1)} %copy-done.6, bf16[320,896]{1,0:T(8,128)(2,1)S(1)} %collective-permute-done.9.refs_0_, bf16[7168,128]{1,0:T(8,128)(2,1)S(1)} %bitcast.21, bf16[7168,128]{1,0:T(8,128)(2,1)S(1)} %bitcast.30, bf16[7168,128]{1,0:T(8,128)(2,1)S(1)} %copy-done.3, ...), custom_call_target="tpu_custom_call" | custom-call | flops 293601280 | bytes 2146304 | tf_op jit(solution)/shard_map/pallas_call | solution.py:113
  98.5 0.0 copy-start.12
  98.5 3.7 %all-to-all-start.1 = ((bf16[8,320,256]{2,1,0:T(8,128)(2,1)}), bf16[8,320,256]{2,1,0:T(8,128)(2,1)S(1)}, u32[]{:S(2)}, u32[]{:S(2)}) async-start(bf16[8,320,256]{2,1,0:T(8,128)(2,1)} %shard_map.68), calls=%async_computation.1 | async-start | bytes 2621440 | tf_op jit(solution)/shard_map/all_to_all | solution.py:217
  102.2 0.0 copy-done.12
  102.2 0.0 copy-start.9
  102.2 0.0 copy-start.11
  102.3 8.2 %collective-permute-start.10 = (bf16[448,2048]{1,0:T(8,128)(2,1)S(1)}, bf16[448,2048]{1,0:T(8,128)(2,1)}, u32[]{:S(2)}, u32[]{:S(2)}) collective-permute-start(bf16[448,2048]{1,0:T(8,128)(2,1)S(1)} %bitcast.41), channel_id=1, source_target_pairs={{0,1},{1,0},{2,3},{3,2},{4,5},{5,4},{6,7},{7,6},{8,9},{9,8},{10,11... | collective-permute-start | bytes 5505032 | tf_op jit(solution)/shard_map/ppermute | solution.py:214
  110.5 3.5 %collective-permute-done.10.other_ref = bf16[448,2048]{1,0:T(8,128)(2,1)} collective-permute-done((bf16[448,2048]{1,0:T(8,128)(2,1)S(1)}, bf16[448,2048]{1,0:T(8,128)(2,1)}, u32[]{:S(2)}, u32[]{:S(2)}) %collective-permute-start.10) | collective-permute-done | bytes 1835040 | tf_op jit(solution)/shard_map/ppermute | solution.py:214
  114.0 18.1 %all-to-all-done.1.hidden_ref = bf16[8,320,256]{2,1,0:T(8,128)(2,1)S(1)} async-done(((bf16[8,320,256]{2,1,0:T(8,128)(2,1)}), bf16[8,320,256]{2,1,0:T(8,128)(2,1)S(1)}, u32[]{:S(2)}, u32[]{:S(2)}) %all-to-all-start.1) | async-done | bytes 1310752 | tf_op jit(solution)/shard_map/all_to_all | solution.py:217
  132.1 3.5 %shard_map.69 = bf16[4,2,80,448]{3,2,1,0:T(8,128)(2,1)S(1)} custom-call(s32[1]{0:T(128)} %bitcast.core_ref, bf16[8,320,256]{2,1,0:T(8,128)(2,1)S(1)} %all-to-all-done.1.hidden_ref, bf16[448,2048]{1,0:T(8,128)(2,1)} %bitcast.40, bf16[448,2048]{1,0:T(8,128)(2,1)} %collective-permute-done.10.other_ref), custom_call_target="tpu_custom_call" | custom-call | flops 1174405120 | bytes 6000000 | tf_op jit(solution)/shard_map/pallas_call | solution.py:156
  135.6 19.1 %all_to_all.16 = bf16[8,80,448]{2,1,0:T(8,128)(2,1)S(1)} all-to-all(bf16[8,80,448]{2,1,0:T(8,128)(2,1)S(1)} %bitcast.31), channel_id=1, replica_groups=mesh['dp'=16,'node'=4,'y'=8,'core'=2] {'node','core'}, dimensions={0} | all-to-all | bytes 1146880 | tf_op jit(solution)/shard_map/all_to_all | solution.py:217
  154.6 0.0 copy-done.9
  154.6 0.0 copy-done.11
  154.6 1.3 shard_map.70
  (1 shorter events, 0.0 us)
Async XLA Ops:
  0.0 17.4 %collective-permute-start = (bf16[448,256]{1,0:T(8,128)(2,1)}, bf16[448,256]{1,0:T(8,128)(2,1)S(1)}, u32[]{:S(2)}, u32[]{:S(2)}) collective-permute-start(bf16[448,256]{1,0:T(8,128)(2,1)} %bitcast.36), channel_id=1, source_target_pairs={{0,1},{1,0},{2,3},{3,2},{4,5},{5,4},{6,7},{7,6},{8,9},{9,8},{10,11... | collective-permute-start | bytes 688136 | tf_op jit(solution)/shard_map/ppermute | solution.py:214
  17.4 0.9 copy-start.7
  18.3 0.7 copy-start.8
  19.7 34.6 %copy-start.10 = (s32[2,256]{1,0:T(2,128)}, s32[2,256]{1,0:T(2,128)S(1)}, u32[]{:S(2)}) copy-start(s32[2,256]{1,0:T(2,128)S(1)} %get-tuple-element.22.pick_ref) | copy-start | bytes 6148
  19.7 36.6 %collective-permute-start.6 = (bf16[7168,128]{1,0:T(8,128)(2,1)}, bf16[7168,128]{1,0:T(8,128)(2,1)S(1)}, u32[]{:S(2)}, u32[]{:S(2)}) collective-permute-start(bf16[7168,128]{1,0:T(8,128)(2,1)} %bitcast.13), channel_id=1, source_target_pairs={{0,1},{1,0},{2,3},{3,2},{4,5},{5,4},{6,7},{7,6},{8,9},{9,8},{10,11... | collective-permute-start | bytes 5505032 | tf_op jit(solution)/shard_map/ppermute | solution.py:214
  22.0 34.3 %collective-permute-start.7 = (bf16[7168,128]{1,0:T(8,128)(2,1)}, bf16[7168,128]{1,0:T(8,128)(2,1)}, u32[]{:S(2)}, u32[]{:S(2)}) collective-permute-start(bf16[7168,128]{1,0:T(8,128)(2,1)} %bitcast.22), channel_id=1, source_target_pairs={{0,1},{1,0},{2,3},{3,2},{4,5},{5,4},{6,7},{7,6},{8,9},{9,8},{10,11... | collective-permute-start | bytes 5505032 | tf_op jit(solution)/shard_map/ppermute | solution.py:214
  35.9 15.0 %collective-permute-start.4 = (bf16[320,896]{1,0:T(8,128)(2,1)S(1)}, bf16[320,896]{1,0:T(8,128)(2,1)}, u32[]{:S(2)}, u32[]{:S(2)}) collective-permute-start(bf16[320,896]{1,0:T(8,128)(2,1)S(1)} %bitcast.32), channel_id=1, source_target_pairs={{0,14},{2,0},{4,2},{6,4},{8,6},{10,8},{12,10},{14,12},{1,15},{3,1}... | collective-permute-start | bytes 1720328 | tf_op jit(solution)/shard_map/ppermute | solution.py:211
  37.9 16.5 %collective-permute-start.1 = (bf16[320,896]{1,0:T(8,128)(2,1)S(1)}, bf16[320,896]{1,0:T(8,128)(2,1)}, u32[]{:S(2)}, u32[]{:S(2)}) collective-permute-start(bf16[320,896]{1,0:T(8,128)(2,1)S(1)} %bitcast.33), channel_id=1, source_target_pairs={{0,2},{2,4},{4,6},{6,8},{8,10},{10,12},{12,14},{14,0},{1,3},{3,5},... | collective-permute-start | bytes 1720328 | tf_op jit(solution)/shard_map/ppermute | solution.py:211
  50.9 14.1 %collective-permute-start.5 = (bf16[320,896]{1,0:T(8,128)(2,1)}, bf16[320,896]{1,0:T(8,128)(2,1)S(1)}, u32[]{:S(2)}, u32[]{:S(2)}) collective-permute-start(bf16[320,896]{1,0:T(8,128)(2,1)} %collective-permute-done.4.refs_2_), channel_id=1, source_target_pairs={{0,14},{2,0},{4,2},{6,4},{8,6},{10,8},{12,10},{14,12},{1,15},{3,1}... | collective-permute-start | bytes 1720328 | tf_op jit(solution)/shard_map/ppermute | solution.py:211
  54.3 15.6 %collective-permute-start.2 = (bf16[320,896]{1,0:T(8,128)(2,1)}, bf16[320,896]{1,0:T(8,128)(2,1)S(1)}, u32[]{:S(2)}, u32[]{:S(2)}) collective-permute-start(bf16[320,896]{1,0:T(8,128)(2,1)} %collective-permute-done.1.refs_1_), channel_id=1, source_target_pairs={{0,2},{2,4},{4,6},{6,8},{8,10},{10,12},{12,14},{14,0},{1,3},{3,5},... | collective-permute-start | bytes 1720328 | tf_op jit(solution)/shard_map/ppermute | solution.py:211
  56.4 1.2 copy-start.2
  62.1 0.5 copy-start.5
  65.1 14.1 %collective-permute-start.8 = (bf16[320,896]{1,0:T(8,128)(2,1)S(1)}, bf16[320,896]{1,0:T(8,128)(2,1)S(1)}, u32[]{:S(2)}, u32[]{:S(2)}) collective-permute-start(bf16[320,896]{1,0:T(8,128)(2,1)S(1)} %collective-permute-done.5.refs_1_), channel_id=1, source_target_pairs={{0,14},{2,0},{4,2},{6,4},{8,6},{10,8},{12,10},{14,12},{1,15},{3,1}... | collective-permute-start | bytes 1720328 | tf_op jit(solution)/shard_map/ppermute | solution.py:211
  70.0 14.2 %collective-permute-start.3 = (bf16[320,896]{1,0:T(8,128)(2,1)S(1)}, bf16[320,896]{1,0:T(8,128)(2,1)S(1)}, u32[]{:S(2)}, u32[]{:S(2)}) collective-permute-start(bf16[320,896]{1,0:T(8,128)(2,1)S(1)} %collective-permute-done.2.refs_0_), channel_id=1, source_target_pairs={{0,2},{2,4},{4,6},{6,8},{8,10},{10,12},{12,14},{14,0},{1,3},{3,5},... | collective-permute-start | bytes 1720328 | tf_op jit(solution)/shard_map/ppermute | solution.py:211
  71.9 1.1 copy-start.4
  73.0 0.6 copy-start.6
  84.3 11.0 %copy-start = (bf16[1,7168,128]{2,1,0:T(8,128)(2,1)S(1)}, bf16[1,7168,128]{2,1,0:T(8,128)(2,1)}, u32[]{:S(2)}) copy-start(bf16[1,7168,128]{2,1,0:T(8,128)(2,1)} %param.9) | copy-start | bytes 5505028
  84.3 11.0 %copy-start.1 = (bf16[1,7168,128]{2,1,0:T(8,128)(2,1)S(1)}, bf16[1,7168,128]{2,1,0:T(8,128)(2,1)}, u32[]{:S(2)}) copy-start(bf16[1,7168,128]{2,1,0:T(8,128)(2,1)} %param.10) | copy-start | bytes 5505028
  84.3 11.0 %copy-start.3 = (bf16[7168,128]{1,0:T(8,128)(2,1)S(1)}, bf16[7168,128]{1,0:T(8,128)(2,1)}, u32[]{:S(2)}) copy-start(bf16[7168,128]{1,0:T(8,128)(2,1)} %copy-done.2) | copy-start | bytes 5505028
  84.3 11.0 %collective-permute-start.9 = (bf16[320,896]{1,0:T(8,128)(2,1)S(1)}, bf16[320,896]{1,0:T(8,128)(2,1)S(1)}, u32[]{:S(2)}, u32[]{:S(2)}) collective-permute-start(bf16[320,896]{1,0:T(8,128)(2,1)S(1)} %broadcast_select_fusion), channel_id=1, source_target_pairs={{0,2},{1,15},{2,4},{3,1},{4,6},{5,3},{6,8},{7,5},{8,10},{9,7},{10,... | collective-permute-start | bytes 1720328 | tf_op jit(solution)/shard_map/ppermute | solution.py:235
  98.5 3.7 %copy-start.12 = (bf16[1,2048,448]{1,2,0:T(8,128)(2,1)S(1)}, bf16[1,2048,448]{1,2,0:T(8,128)(2,1)}, u32[]{:S(2)}) copy-start(bf16[1,2048,448]{1,2,0:T(8,128)(2,1)} %param.11) | copy-start | bytes 5505028
  98.5 33.6 %all-to-all-start.1 = ((bf16[8,320,256]{2,1,0:T(8,128)(2,1)}), bf16[8,320,256]{2,1,0:T(8,128)(2,1)S(1)}, u32[]{:S(2)}, u32[]{:S(2)}) async-start(bf16[8,320,256]{2,1,0:T(8,128)(2,1)} %shard_map.68), calls=%async_computation.1 | async-start | bytes 2621440 | tf_op jit(solution)/shard_map/all_to_all | solution.py:217
  102.2 52.4 %copy-start.9 = (f32[256,2]{0,1:T(2,128)S(1)}, f32[256,2]{0,1:T(2,128)}, u32[]{:S(2)}) copy-start(f32[256,2]{0,1:T(2,128)} %param.8) | copy-start | bytes 6148
  102.2 52.4 %copy-start.11 = (s32[2,256]{1,0:T(2,128)S(1)}, s32[2,256]{1,0:T(2,128)}, u32[]{:S(2)}) copy-start(s32[2,256]{1,0:T(2,128)} %copy-done.10) | copy-start | bytes 6148
  102.3 11.8 %collective-permute-start.10 = (bf16[448,2048]{1,0:T(8,128)(2,1)S(1)}, bf16[448,2048]{1,0:T(8,128)(2,1)}, u32[]{:S(2)}, u32[]{:S(2)}) collective-permute-start(bf16[448,2048]{1,0:T(8,128)(2,1)S(1)} %bitcast.41), channel_id=1, source_target_pairs={{0,1},{1,0},{2,3},{3,2},{4,5},{5,4},{6,7},{7,6},{8,9},{9,8},{10,11... | collective-permute-start | bytes 5505032 | tf_op jit(solution)/shard_map/ppermute | solution.py:214
where the time goes:
time: 157 us; the launch traced here: 156 us
  starting transfers between devices  52 us (33%)
  waiting for transfers between devices  48.5 us (31%)
  blocking collectives  30.9 us (20%)
  Pallas kernels  19 us (12%)
  local copies, waits for them, and re-layouts  5.08 us (3%)
    all_to_all x2, blocking collectives, exchange(): return lax.all_to_all(x, axes, split_axis=0, concat_axis=0, tiled=True)  30.9 us
    ppermute x4, starting transfers between devices, across(): return lax.ppermute(x, 'core', SWAP)  28.6 us
    ppermute x6, waiting for transfers between devices, hop(): lax.ppermute(x, 'y', [(i, (i + distance) % chips) for i in range(chips)])  19.8 us
    all_to_all x1, waiting for transfers between devices, exchange(): return lax.all_to_all(x, axes, split_axis=0, concat_axis=0, tiled=True)  18.1 us
    ppermute x6, starting transfers between devices, hop(): lax.ppermute(x, 'y', [(i, (i + distance) % chips) for i in range(chips)])  17.4 us
    pallas_call x4, Pallas kernels, gate_up(): pl.pallas_call(functools.partial(gate_up_kernel, tuple((len(blocks) for b...  13.5 us
    ppermute x1, waiting for transfers between devices, local(): lax.ppermute(jnp.where(core[0] == 0, up_y, down_y), ('y', 'core'), pairs)  5.8 us
    unnamed x26, local copies, waits for them, and re-layouts  5.08 us
  transfers between devices with their start and end apart: 12, of which 8 were waited for; matrix products, arithmetic and copies ran while one was open for 0% of the time, Pallas kernels for 7%

commit v1 on v0

--- a/solution.py
+++ b/solution.py
@@ -225,14 +225,16 @@
 
     up_y, down_y = hop(rows, 1), hop(rows, -1)
     sums = gate_up([((rows,), 0), ((up_y,), chips - 1), ((down_y,), 1)], None, weights, idx)
+    far = None
     for s in range(2, chips // 2):
         up_y, down_y = hop(up_y, 1), hop(down_y, -1)
         new = gate_up([((up_y,), chips - s), ((down_y,), s)], sums, weights, idx)
-        down_y, sums = lax.optimization_barrier((down_y, sums))
+        if s == chips // 2 - 2:
+            pairs = [(y, side) for y in range(chips) for side in range(2)]
+            pairs = [(2 * y + side, 2 * ((y + 2 - 4 * side) % chips) + side) for y, side in pairs]
+            far = lax.ppermute(jnp.where(core[0] == 0, up_y, down_y), ("y", "core"), pairs)
+            down_y, sums = lax.optimization_barrier((down_y, sums))
         sums = new
-    pairs = [(y, side) for y in range(chips) for side in range(2)]
-    pairs = [(2 * y + side, 2 * ((y + 1 - 2 * side) % chips) + side) for y, side in pairs]
-    far = lax.ppermute(jnp.where(core[0] == 0, up_y, down_y), ("y", "core"), pairs)
     hidden = gate_up([((far,), chips // 2)], sums, weights, idx, last=chips)
     hidden, down_w = lax.optimization_barrier((hidden, w_down[0].T))
     hidden, down_other = exchange(hidden, "y"), across(down_w)

time: 157 us -> 168 us (1.070)
  waiting for transfers between devices: 48.5 us -> 69.9 us
  blocking collectives: 30.9 us -> 25.8 us
  starting transfers between devices: 52 us -> 49.2 us
  local copies, waits for them, and re-layouts: 5.08 us -> 2.87 us
    all_to_all x1, waiting for transfers between devices: 18.1 us -> 29 us  [exchange(): return lax.all_to_all(x, axes, split_axis=0, concat_axis=0, tiled=True)]
    ppermute x1, waiting for transfers between devices: 5.8 us -> 13.1 us  [local(): lax.ppermute(jnp.where(core[0] == 0, up_y, down_y), ('y', 'core'), pairs)]
    ppermute x4, starting transfers between devices: 28.6 us -> 22.3 us  [across(): return lax.ppermute(x, 'core', SWAP)]
    all_to_all x2, blocking collectives: 30.9 us -> 25.8 us  [exchange(): return lax.all_to_all(x, axes, split_axis=0, concat_axis=0, tiled=True)]
    ppermute x6, waiting for transfers between devices: 19.8 us -> 22.6 us  [hop(): lax.ppermute(x, 'y', [(i, (i + distance) % chips) for i in range(chips)])]
    unnamed x26 -> x22, local copies, waits for them, and re-layouts: 5.08 us -> 2.87 us
    ppermute x6, starting transfers between devices: 17.4 us -> 19.6 us  [hop(): lax.ppermute(x, 'y', [(i, (i + distance) % chips) for i in range(chips)])]
    all_to_all x1, starting transfers between devices: 3.7 us -> 5.43 us  [exchange(): return lax.all_to_all(x, axes, split_axis=0, concat_axis=0, tiled=True)]
  transfers between devices with their start and end apart: 12 -> 12, of which waited for: 8 -> 7; matrix products, arithmetic and copies ran while one was open for 0% -> 0% of each run, Pallas kernels for 7% -> 6%
where the time goes in v1:
time: 168 us; the launch traced here: 167 us
  waiting for transfers between devices  69.9 us (42%)
  starting transfers between devices  49.2 us (29%)
  blocking collectives  25.8 us (15%)
  Pallas kernels  19 us (11%)
  local copies, waits for them, and re-layouts  2.87 us (2%)
    all_to_all x1, waiting for transfers between devices, exchange(): return lax.all_to_all(x, axes, split_axis=0, concat_axis=0, tiled=True)  29 us
    all_to_all x2, blocking collectives, exchange(): return lax.all_to_all(x, axes, split_axis=0, concat_axis=0, tiled=True)  25.8 us
    ppermute x6, waiting for transfers between devices, hop(): lax.ppermute(x, 'y', [(i, (i + distance) % chips) for i in range(chips)])  22.6 us
    ppermute x4, starting transfers between devices, across(): return lax.ppermute(x, 'core', SWAP)  22.3 us
    ppermute x6, starting transfers between devices, hop(): lax.ppermute(x, 'y', [(i, (i + distance) % chips) for i in range(chips)])  19.6 us
    pallas_call x4, Pallas kernels, gate_up(): pl.pallas_call(functools.partial(gate_up_kernel, tuple((len(blocks) for b...  13.5 us
    ppermute x1, waiting for transfers between devices, local(): lax.ppermute(jnp.where(core[0] == 0, up_y, down_y), ('y', 'core'), pairs)  13.1 us
    all_to_all x1, starting transfers between devices, exchange(): return lax.all_to_all(x, axes, split_axis=0, concat_axis=0, tiled=True)  5.43 us
  transfers between devices with their start and end apart: 12, of which 7 were waited for; matrix products, arithmetic and copies ran while one was open for 0% of the time, Pallas kernels for 6%

profile of v1, /device:TPU:1, one launch (start us, length us, event | category | flops | bytes accessed | tf_op | source)
XLA Modules:
  0.0 167.2 jit_solution(1350010179289409902)
XLA Ops:
  0.0 16.1 %collective-permute-start = (bf16[448,256]{1,0:T(8,128)(2,1)}, bf16[448,256]{1,0:T(8,128)(2,1)S(1)}, u32[]{:S(2)}, u32[]{:S(2)}) collective-permute-start(bf16[448,256]{1,0:T(8,128)(2,1)} %bitcast.36), channel_id=1, source_target_pairs={{0,1},{1,0},{2,3},{3,2},{4,5},{5,4},{6,7},{7,6},{8,9},{9,8},{10,11... | collective-permute-start | bytes 688136 | tf_op jit(solution)/shard_map/ppermute | solution.py:214
  16.1 1.3 collective-permute-done.other_ref
  17.4 0.0 copy-start.5
  17.4 0.9 copy-done.5
  18.3 0.0 copy-start.6
  18.3 0.7 copy-done.6
  19.0 0.8 shard_map.64
  19.7 0.0 copy-start.8
  19.7 2.3 %collective-permute-start.6 = (bf16[7168,128]{1,0:T(8,128)(2,1)}, bf16[7168,128]{1,0:T(8,128)(2,1)S(1)}, u32[]{:S(2)}, u32[]{:S(2)}) collective-permute-start(bf16[7168,128]{1,0:T(8,128)(2,1)} %bitcast.13), channel_id=1, source_target_pairs={{0,1},{1,0},{2,3},{3,2},{4,5},{5,4},{6,7},{7,6},{8,9},{9,8},{10,11... | collective-permute-start | bytes 5505032 | tf_op jit(solution)/shard_map/ppermute | solution.py:214
  22.0 2.0 %collective-permute-start.7 = (bf16[7168,128]{1,0:T(8,128)(2,1)}, bf16[7168,128]{1,0:T(8,128)(2,1)}, u32[]{:S(2)}, u32[]{:S(2)}) collective-permute-start(bf16[7168,128]{1,0:T(8,128)(2,1)} %bitcast.22), channel_id=1, source_target_pairs={{0,1},{1,0},{2,3},{3,2},{4,5},{5,4},{6,7},{7,6},{8,9},{9,8},{10,11... | collective-permute-start | bytes 5505032 | tf_op jit(solution)/shard_map/ppermute | solution.py:214
  24.1 11.8 %all_to_all.15 = bf16[4,80,896]{2,1,0:T(8,128)(2,1)S(1)} all-to-all(bf16[4,80,896]{2,1,0:T(8,128)(2,1)S(1)} %get-tuple-element.14), channel_id=1, replica_groups=mesh['dp'=16,'node'=4,'y'=8,'core'=2] {'node'}, dimensions={0} | all-to-all | bytes 1146880 | tf_op jit(solution)/shard_map/all_to_all | solution.py:217
  35.9 1.9 %collective-permute-start.1 = (bf16[320,896]{1,0:T(8,128)(2,1)S(1)}, bf16[320,896]{1,0:T(8,128)(2,1)}, u32[]{:S(2)}, u32[]{:S(2)}) collective-permute-start(bf16[320,896]{1,0:T(8,128)(2,1)S(1)} %bitcast.32), channel_id=1, source_target_pairs={{0,2},{2,4},{4,6},{6,8},{8,10},{10,12},{12,14},{14,0},{1,3},{3,5},... | collective-permute-start | bytes 1720328 | tf_op jit(solution)/shard_map/ppermute | solution.py:211
  37.9 4.6 %collective-permute-start.3 = (bf16[320,896]{1,0:T(8,128)(2,1)S(1)}, bf16[320,896]{1,0:T(8,128)(2,1)}, u32[]{:S(2)}, u32[]{:S(2)}) collective-permute-start(bf16[320,896]{1,0:T(8,128)(2,1)S(1)} %bitcast.33), channel_id=1, source_target_pairs={{0,14},{2,0},{4,2},{6,4},{8,6},{10,8},{12,10},{14,12},{1,15},{3,1}... | collective-permute-start | bytes 1720328 | tf_op jit(solution)/shard_map/ppermute | solution.py:211
  42.4 9.7 %collective-permute-done.1.refs_1_ = bf16[320,896]{1,0:T(8,128)(2,1)} collective-permute-done((bf16[320,896]{1,0:T(8,128)(2,1)S(1)}, bf16[320,896]{1,0:T(8,128)(2,1)}, u32[]{:S(2)}, u32[]{:S(2)}) %collective-permute-start.1) | collective-permute-done | bytes 573472 | tf_op jit(solution)/shard_map/ppermute | solution.py:211
  52.1 1.9 %collective-permute-start.2 = (bf16[320,896]{1,0:T(8,128)(2,1)}, bf16[320,896]{1,0:T(8,128)(2,1)S(1)}, u32[]{:S(2)}, u32[]{:S(2)}) collective-permute-start(bf16[320,896]{1,0:T(8,128)(2,1)} %collective-permute-done.1.refs_1_), channel_id=1, source_target_pairs={{0,2},{2,4},{4,6},{6,8},{8,10},{10,12},{12,14},{14,0},{1,3},{3,5},... | collective-permute-start | bytes 1720328 | tf_op jit(solution)/shard_map/ppermute | solution.py:211
  54.0 0.0 collective-permute-done.3.refs_2_
  54.0 0.0 copy-done.8
  54.1 4.6 %collective-permute-start.4 = (bf16[320,896]{1,0:T(8,128)(2,1)}, bf16[320,896]{1,0:T(8,128)(2,1)S(1)}, u32[]{:S(2)}, u32[]{:S(2)}) collective-permute-start(bf16[320,896]{1,0:T(8,128)(2,1)} %collective-permute-done.3.refs_2_), channel_id=1, source_target_pairs={{0,14},{2,0},{4,2},{6,4},{8,6},{10,8},{12,10},{14,12},{1,15},{3,1}... | collective-permute-start | bytes 1720328 | tf_op jit(solution)/shard_map/ppermute | solution.py:211
  58.7 0.1 pad_add_fusion.idx_ref
  58.7 8.7 %collective-permute-done.2.refs_0_ = bf16[320,896]{1,0:T(8,128)(2,1)S(1)} collective-permute-done((bf16[320,896]{1,0:T(8,128)(2,1)}, bf16[320,896]{1,0:T(8,128)(2,1)S(1)}, u32[]{:S(2)}, u32[]{:S(2)}) %collective-permute-start.2) | collective-permute-done | bytes 573472 | tf_op jit(solution)/shard_map/ppermute | solution.py:211
  67.5 1.9 %collective-permute-start.8 = (bf16[320,896]{1,0:T(8,128)(2,1)S(1)}, bf16[320,896]{1,0:T(8,128)(2,1)S(1)}, u32[]{:S(2)}, u32[]{:S(2)}) collective-permute-start(bf16[320,896]{1,0:T(8,128)(2,1)S(1)} %collective-permute-done.2.refs_0_), channel_id=1, source_target_pairs={{0,2},{2,4},{4,6},{6,8},{8,10},{10,12},{12,14},{14,0},{1,3},{3,5},... | collective-permute-start | bytes 1720328 | tf_op jit(solution)/shard_map/ppermute | solution.py:211
  69.4 0.0 collective-permute-done.6.refs_5_.refs_9_.refs_13_.refs_4_.refs_8_.refs_3_
  69.4 0.0 copy-start.2
  69.4 0.0 collective-permute-done.7.refs_6_.refs_10_.refs_14_.refs_5_.refs_9_.refs_4_
  69.4 1.2 copy-done.2
  70.6 4.5 %shard_map.65.refs_10_ = f32[320,512]{1,0:T(8,128)} custom-call(s32[9]{0:T(128)S(1)} %pad_add_fusion.idx_ref, bf16[320,896]{1,0:T(8,128)(2,1)S(1)} %bitcast.34, bf16[320,896]{1,0:T(8,128)(2,1)} %collective-permute-done.1.refs_1_, bf16[320,896]{1,0:T(8,128)(2,1)} %collective-permute-done.3.refs_2_, bf16[7168,128]{1,0:T(8,128)(2,1)} %bitcast.14, ...), custom_call_target="tpu_custom_call" | custom-call | flops 880803840 | bytes 5128192 | tf_op jit(solution)/shard_map/pallas_call | solution.py:113
  75.2 0.0 copy-start.4
  75.2 0.0 collective-permute-done.4.refs_1_
  75.2 4.7 %collective-permute-start.9 = (bf16[320,896]{1,0:T(8,128)(2,1)S(1)}, bf16[320,896]{1,0:T(8,128)(2,1)S(1)}, u32[]{:S(2)}, u32[]{:S(2)}) collective-permute-start(bf16[320,896]{1,0:T(8,128)(2,1)S(1)} %collective-permute-done.4.refs_1_), channel_id=1, source_target_pairs={{0,14},{2,0},{4,2},{6,4},{8,6},{10,8},{12,10},{14,12},{1,15},{3,1}... | collective-permute-start | bytes 1720328 | tf_op jit(solution)/shard_map/ppermute | solution.py:211
  79.9 0.1 broadcast_select_fusion
  80.0 1.9 %collective-permute-start.5 = (bf16[320,896]{1,0:T(8,128)(2,1)S(1)}, bf16[320,896]{1,0:T(8,128)(2,1)S(1)}, u32[]{:S(2)}, u32[]{:S(2)}) collective-permute-start(bf16[320,896]{1,0:T(8,128)(2,1)S(1)} %broadcast_select_fusion), channel_id=1, source_target_pairs={{0,4},{1,13},{2,6},{3,15},{4,8},{5,1},{6,10},{7,3},{8,12},{9,5},{1... | collective-permute-start | bytes 1720328 | tf_op jit(solution)/shard_map/ppermute | solution.py:235
  81.9 0.0 copy-done.4
  81.9 2.9 %shard_map.66.refs_10_ = f32[320,512]{1,0:T(8,128)S(1)} custom-call(s32[9]{0:T(128)S(1)} %pad_add_fusion.idx_ref, bf16[320,896]{1,0:T(8,128)(2,1)S(1)} %collective-permute-done.2.refs_0_, bf16[320,896]{1,0:T(8,128)(2,1)S(1)} %collective-permute-done.4.refs_1_, bf16[7168,128]{1,0:T(8,128)(2,1)} %bitcast.17, ...), custom_call_target="tpu_custom_call", output_to_operand_aliasing={{}: (11, {})} | custom-call | flops 587202560 | bytes 3637248 | tf_op jit(solution)/shard_map/pallas_call | solution.py:113
  84.8 0.0 copy-start
  84.8 0.0 copy-start.1
  84.8 0.0 copy-start.3
  84.8 0.0 collective-permute-done.8.refs_0_
  84.8 4.2 %collective-permute-done.9.refs_1_ = bf16[320,896]{1,0:T(8,128)(2,1)S(1)} collective-permute-done((bf16[320,896]{1,0:T(8,128)(2,1)S(1)}, bf16[320,896]{1,0:T(8,128)(2,1)S(1)}, u32[]{:S(2)}, u32[]{:S(2)}) %collective-permute-start.9) | collective-permute-done | bytes 573472 | tf_op jit(solution)/shard_map/ppermute | solution.py:211
  89.0 2.9 %shard_map.67.refs_5_ = f32[320,512]{1,0:T(8,128)S(1)} custom-call(s32[9]{0:T(128)S(1)} %pad_add_fusion.idx_ref, bf16[320,896]{1,0:T(8,128)(2,1)S(1)} %collective-permute-done.8.refs_0_, bf16[320,896]{1,0:T(8,128)(2,1)S(1)} %collective-permute-done.9.refs_1_, bf16[7168,128]{1,0:T(8,128)(2,1)} %bitcast.19, ...), custom_call_target="tpu_custom_call", output_to_operand_aliasing={{}: (11, {})} | custom-call | flops 587202560 | bytes 3637248 | tf_op jit(solution)/shard_map/pallas_call | solution.py:113
  91.9 13.1 %collective-permute-done.5.refs_0_ = bf16[320,896]{1,0:T(8,128)(2,1)S(1)} collective-permute-done((bf16[320,896]{1,0:T(8,128)(2,1)S(1)}, bf16[320,896]{1,0:T(8,128)(2,1)S(1)}, u32[]{:S(2)}, u32[]{:S(2)}) %collective-permute-start.5) | collective-permute-done | bytes 573472 | tf_op jit(solution)/shard_map/ppermute | solution.py:235
  104.9 0.0 copy-done
  104.9 0.0 copy-done.1
  104.9 0.0 copy-done.3
  104.9 3.2 %shard_map.68 = bf16[8,320,256]{2,1,0:T(8,128)(2,1)} custom-call(s32[9]{0:T(128)S(1)} %pad_add_fusion.idx_ref, bf16[320,896]{1,0:T(8,128)(2,1)S(1)} %collective-permute-done.5.refs_0_, bf16[7168,128]{1,0:T(8,128)(2,1)S(1)} %bitcast.21, bf16[7168,128]{1,0:T(8,128)(2,1)S(1)} %bitcast.30, bf16[7168,128]{1,0:T(8,128)(2,1)S(1)} %copy-done.3, ...), custom_call_target="tpu_custom_call" | custom-call | flops 293601280 | bytes 2146304 | tf_op jit(solution)/shard_map/pallas_call | solution.py:113
  108.1 0.0 copy-start.10
  108.1 5.4 %all-to-all-start.1 = ((bf16[8,320,256]{2,1,0:T(8,128)(2,1)}), bf16[8,320,256]{2,1,0:T(8,128)(2,1)S(1)}, u32[]{:S(2)}, u32[]{:S(2)}) async-start(bf16[8,320,256]{2,1,0:T(8,128)(2,1)} %shard_map.68), calls=%async_computation.1 | async-start | bytes 2621440 | tf_op jit(solution)/shard_map/all_to_all | solution.py:217
  113.6 0.0 copy-done.10
  113.6 0.0 copy-start.7
  113.6 0.0 copy-start.9
  113.6 1.9 %collective-permute-start.10 = (bf16[448,2048]{1,0:T(8,128)(2,1)S(1)}, bf16[448,2048]{1,0:T(8,128)(2,1)}, u32[]{:S(2)}, u32[]{:S(2)}) collective-permute-start(bf16[448,2048]{1,0:T(8,128)(2,1)S(1)} %bitcast.41), channel_id=1, source_target_pairs={{0,1},{1,0},{2,3},{3,2},{4,5},{5,4},{6,7},{7,6},{8,9},{9,8},{10,11... | collective-permute-start | bytes 5505032 | tf_op jit(solution)/shard_map/ppermute | solution.py:214
  115.5 3.9 %collective-permute-done.10.other_ref = bf16[448,2048]{1,0:T(8,128)(2,1)} collective-permute-done((bf16[448,2048]{1,0:T(8,128)(2,1)S(1)}, bf16[448,2048]{1,0:T(8,128)(2,1)}, u32[]{:S(2)}, u32[]{:S(2)}) %collective-permute-start.10) | collective-permute-done | bytes 1835040 | tf_op jit(solution)/shard_map/ppermute | solution.py:214
  119.4 29.0 %all-to-all-done.1.hidden_ref = bf16[8,320,256]{2,1,0:T(8,128)(2,1)S(1)} async-done(((bf16[8,320,256]{2,1,0:T(8,128)(2,1)}), bf16[8,320,256]{2,1,0:T(8,128)(2,1)S(1)}, u32[]{:S(2)}, u32[]{:S(2)}) %all-to-all-start.1) | async-done | bytes 1310752 | tf_op jit(solution)/shard_map/all_to_all | solution.py:217
  148.5 3.5 %shard_map.69 = bf16[4,2,80,448]{3,2,1,0:T(8,128)(2,1)S(1)} custom-call(s32[1]{0:T(128)} %bitcast.core_ref, bf16[8,320,256]{2,1,0:T(8,128)(2,1)S(1)} %all-to-all-done.1.hidden_ref, bf16[448,2048]{1,0:T(8,128)(2,1)} %bitcast.40, bf16[448,2048]{1,0:T(8,128)(2,1)} %collective-permute-done.10.other_ref), custom_call_target="tpu_custom_call" | custom-call | flops 1174405120 | bytes 6000000 | tf_op jit(solution)/shard_map/pallas_call | solution.py:156
  151.9 14.0 %all_to_all.16 = bf16[8,80,448]{2,1,0:T(8,128)(2,1)S(1)} all-to-all(bf16[8,80,448]{2,1,0:T(8,128)(2,1)S(1)} %bitcast.31), channel_id=1, replica_groups=mesh['dp'=16,'node'=4,'y'=8,'core'=2] {'node','core'}, dimensions={0} | all-to-all | bytes 1146880 | tf_op jit(solution)/shard_map/all_to_all | solution.py:217
  165.9 0.0 copy-done.7
  165.9 0.0 copy-done.9
  165.9 1.3 shard_map.70
  (1 shorter events, 0.0 us)
Async XLA Ops:
  0.0 17.4 %collective-permute-start = (bf16[448,256]{1,0:T(8,128)(2,1)}, bf16[448,256]{1,0:T(8,128)(2,1)S(1)}, u32[]{:S(2)}, u32[]{:S(2)}) collective-permute-start(bf16[448,256]{1,0:T(8,128)(2,1)} %bitcast.36), channel_id=1, source_target_pairs={{0,1},{1,0},{2,3},{3,2},{4,5},{5,4},{6,7},{7,6},{8,9},{9,8},{10,11... | collective-permute-start | bytes 688136 | tf_op jit(solution)/shard_map/ppermute | solution.py:214
  17.4 0.9 copy-start.5
  18.3 0.7 copy-start.6
  19.7 34.3 %copy-start.8 = (s32[2,256]{1,0:T(2,128)}, s32[2,256]{1,0:T(2,128)S(1)}, u32[]{:S(2)}) copy-start(s32[2,256]{1,0:T(2,128)S(1)} %get-tuple-element.20.pick_ref) | copy-start | bytes 6148
  19.7 49.7 %collective-permute-start.6 = (bf16[7168,128]{1,0:T(8,128)(2,1)}, bf16[7168,128]{1,0:T(8,128)(2,1)S(1)}, u32[]{:S(2)}, u32[]{:S(2)}) collective-permute-start(bf16[7168,128]{1,0:T(8,128)(2,1)} %bitcast.13), channel_id=1, source_target_pairs={{0,1},{1,0},{2,3},{3,2},{4,5},{5,4},{6,7},{7,6},{8,9},{9,8},{10,11... | collective-permute-start | bytes 5505032 | tf_op jit(solution)/shard_map/ppermute | solution.py:214
  22.0 47.4 %collective-permute-start.7 = (bf16[7168,128]{1,0:T(8,128)(2,1)}, bf16[7168,128]{1,0:T(8,128)(2,1)}, u32[]{:S(2)}, u32[]{:S(2)}) collective-permute-start(bf16[7168,128]{1,0:T(8,128)(2,1)} %bitcast.22), channel_id=1, source_target_pairs={{0,1},{1,0},{2,3},{3,2},{4,5},{5,4},{6,7},{7,6},{8,9},{9,8},{10,11... | collective-permute-start | bytes 5505032 | tf_op jit(solution)/shard_map/ppermute | solution.py:214
  35.9 16.2 %collective-permute-start.1 = (bf16[320,896]{1,0:T(8,128)(2,1)S(1)}, bf16[320,896]{1,0:T(8,128)(2,1)}, u32[]{:S(2)}, u32[]{:S(2)}) collective-permute-start(bf16[320,896]{1,0:T(8,128)(2,1)S(1)} %bitcast.32), channel_id=1, source_target_pairs={{0,2},{2,4},{4,6},{6,8},{8,10},{10,12},{12,14},{14,0},{1,3},{3,5},... | collective-permute-start | bytes 1720328 | tf_op jit(solution)/shard_map/ppermute | solution.py:211
  37.9 16.2 %collective-permute-start.3 = (bf16[320,896]{1,0:T(8,128)(2,1)S(1)}, bf16[320,896]{1,0:T(8,128)(2,1)}, u32[]{:S(2)}, u32[]{:S(2)}) collective-permute-start(bf16[320,896]{1,0:T(8,128)(2,1)S(1)} %bitcast.33), channel_id=1, source_target_pairs={{0,14},{2,0},{4,2},{6,4},{8,6},{10,8},{12,10},{14,12},{1,15},{3,1}... | collective-permute-start | bytes 1720328 | tf_op jit(solution)/shard_map/ppermute | solution.py:211
  52.1 15.4 %collective-permute-start.2 = (bf16[320,896]{1,0:T(8,128)(2,1)}, bf16[320,896]{1,0:T(8,128)(2,1)S(1)}, u32[]{:S(2)}, u32[]{:S(2)}) collective-permute-start(bf16[320,896]{1,0:T(8,128)(2,1)} %collective-permute-done.1.refs_1_), channel_id=1, source_target_pairs={{0,2},{2,4},{4,6},{6,8},{8,10},{10,12},{12,14},{14,0},{1,3},{3,5},... | collective-permute-start | bytes 1720328 | tf_op jit(solution)/shard_map/ppermute | solution.py:211
  54.1 21.1 %collective-permute-start.4 = (bf16[320,896]{1,0:T(8,128)(2,1)}, bf16[320,896]{1,0:T(8,128)(2,1)S(1)}, u32[]{:S(2)}, u32[]{:S(2)}) collective-permute-start(bf16[320,896]{1,0:T(8,128)(2,1)} %collective-permute-done.3.refs_2_), channel_id=1, source_target_pairs={{0,14},{2,0},{4,2},{6,4},{8,6},{10,8},{12,10},{14,12},{1,15},{3,1}... | collective-permute-start | bytes 1720328 | tf_op jit(solution)/shard_map/ppermute | solution.py:211
  67.5 17.3 %collective-permute-start.8 = (bf16[320,896]{1,0:T(8,128)(2,1)S(1)}, bf16[320,896]{1,0:T(8,128)(2,1)S(1)}, u32[]{:S(2)}, u32[]{:S(2)}) collective-permute-start(bf16[320,896]{1,0:T(8,128)(2,1)S(1)} %collective-permute-done.2.refs_0_), channel_id=1, source_target_pairs={{0,2},{2,4},{4,6},{6,8},{8,10},{10,12},{12,14},{14,0},{1,3},{3,5},... | collective-permute-start | bytes 1720328 | tf_op jit(solution)/shard_map/ppermute | solution.py:211
  69.4 1.2 copy-start.2
  75.2 6.7 %copy-start.4 = (f32[320,512]{1,0:T(8,128)S(1)}, f32[320,512]{1,0:T(8,128)}, u32[]{:S(2)}) copy-start(f32[320,512]{1,0:T(8,128)} %shard_map.65.refs_10_) | copy-start | bytes 1966084
  75.2 13.8 %collective-permute-start.9 = (bf16[320,896]{1,0:T(8,128)(2,1)S(1)}, bf16[320,896]{1,0:T(8,128)(2,1)S(1)}, u32[]{:S(2)}, u32[]{:S(2)}) collective-permute-start(bf16[320,896]{1,0:T(8,128)(2,1)S(1)} %collective-permute-done.4.refs_1_), channel_id=1, source_target_pairs={{0,14},{2,0},{4,2},{6,4},{8,6},{10,8},{12,10},{14,12},{1,15},{3,1}... | collective-permute-start | bytes 1720328 | tf_op jit(solution)/shard_map/ppermute | solution.py:211
  80.0 25.0 %collective-permute-start.5 = (bf16[320,896]{1,0:T(8,128)(2,1)S(1)}, bf16[320,896]{1,0:T(8,128)(2,1)S(1)}, u32[]{:S(2)}, u32[]{:S(2)}) collective-permute-start(bf16[320,896]{1,0:T(8,128)(2,1)S(1)} %broadcast_select_fusion), channel_id=1, source_target_pairs={{0,4},{1,13},{2,6},{3,15},{4,8},{5,1},{6,10},{7,3},{8,12},{9,5},{1... | collective-permute-start | bytes 1720328 | tf_op jit(solution)/shard_map/ppermute | solution.py:235
  84.8 20.2 %copy-start = (bf16[1,7168,128]{2,1,0:T(8,128)(2,1)S(1)}, bf16[1,7168,128]{2,1,0:T(8,128)(2,1)}, u32[]{:S(2)}) copy-start(bf16[1,7168,128]{2,1,0:T(8,128)(2,1)} %param.9) | copy-start | bytes 5505028
  84.8 20.2 %copy-start.1 = (bf16[1,7168,128]{2,1,0:T(8,128)(2,1)S(1)}, bf16[1,7168,128]{2,1,0:T(8,128)(2,1)}, u32[]{:S(2)}) copy-start(bf16[1,7168,128]{2,1,0:T(8,128)(2,1)} %param.10) | copy-start | bytes 5505028
  84.8 20.1 %copy-start.3 = (bf16[7168,128]{1,0:T(8,128)(2,1)S(1)}, bf16[7168,128]{1,0:T(8,128)(2,1)}, u32[]{:S(2)}) copy-start(bf16[7168,128]{1,0:T(8,128)(2,1)} %copy-done.2) | copy-start | bytes 5505028
  108.1 5.4 %copy-start.10 = (bf16[1,2048,448]{1,2,0:T(8,128)(2,1)S(1)}, bf16[1,2048,448]{1,2,0:T(8,128)(2,1)}, u32[]{:S(2)}) copy-start(bf16[1,2048,448]{1,2,0:T(8,128)(2,1)} %param.11) | copy-start | bytes 5505028
  108.1 40.3 %all-to-all-start.1 = ((bf16[8,320,256]{2,1,0:T(8,128)(2,1)}), bf16[8,320,256]{2,1,0:T(8,128)(2,1)S(1)}, u32[]{:S(2)}, u32[]{:S(2)}) async-start(bf16[8,320,256]{2,1,0:T(8,128)(2,1)} %shard_map.68), calls=%async_computation.1 | async-start | bytes 2621440 | tf_op jit(solution)/shard_map/all_to_all | solution.py:217
  113.6 52.4 %copy-start.7 = (f32[256,2]{0,1:T(2,128)S(1)}, f32[256,2]{0,1:T(2,128)}, u32[]{:S(2)}) copy-start(f32[256,2]{0,1:T(2,128)} %param.8) | copy-start | bytes 6148
  113.6 52.4 %copy-start.9 = (s32[2,256]{1,0:T(2,128)S(1)}, s32[2,256]{1,0:T(2,128)}, u32[]{:S(2)}) copy-start(s32[2,256]{1,0:T(2,128)} %copy-done.8) | copy-start | bytes 6148
  113.6 5.8 %collective-permute-start.10 = (bf16[448,2048]{1,0:T(8,128)(2,1)S(1)}, bf16[448,2048]{1,0:T(8,128)(2,1)}, u32[]{:S(2)}, u32[]{:S(2)}) collective-permute-start(bf16[448,2048]{1,0:T(8,128)(2,1)S(1)} %bitcast.41), channel_id=1, source_target_pairs={{0,1},{1,0},{2,3},{3,2},{4,5},{5,4},{6,7},{7,6},{8,9},{9,8},{10,11... | collective-permute-start | bytes 5505032 | tf_op jit(solution)/shard_map/ppermute | solution.py:214

commit v2 on v0

--- a/solution.py
+++ b/solution.py
@@ -225,6 +225,8 @@
 
     up_y, down_y = hop(rows, 1), hop(rows, -1)
     sums = gate_up([((rows,), 0), ((up_y,), chips - 1), ((down_y,), 1)], None, weights, idx)
+    sums, down_w = lax.optimization_barrier((sums, w_down[0].T))
+    down_other = across(down_w)
     for s in range(2, chips // 2):
         up_y, down_y = hop(up_y, 1), hop(down_y, -1)
         new = gate_up([((up_y,), chips - s), ((down_y,), s)], sums, weights, idx)
@@ -232,10 +234,10 @@
         sums = new
     pairs = [(y, side) for y in range(chips) for side in range(2)]
     pairs = [(2 * y + side, 2 * ((y + 1 - 2 * side) % chips) + side) for y, side in pairs]
+    sums, down_other = lax.optimization_barrier((sums, down_other))
     far = lax.ppermute(jnp.where(core[0] == 0, up_y, down_y), ("y", "core"), pairs)
     hidden = gate_up([((far,), chips // 2)], sums, weights, idx, last=chips)
-    hidden, down_w = lax.optimization_barrier((hidden, w_down[0].T))
-    hidden, down_other = exchange(hidden, "y"), across(down_w)
+    hidden = exchange(hidden, "y")
     out = down(core, hidden, down_w, down_other, half)
     back = exchange(out.reshape(2 * nodes, half, width), ("node", "core"))
     return combine(back.reshape(2 * nodes * half, width), pick, route_weight.T).T

time: 157 us -> 158 us (level)
  blocking collectives: 30.9 us -> 62.9 us
  waiting for transfers between devices: 48.5 us -> 26.3 us
  starting transfers between devices: 52 us -> 44.4 us
    all_to_all x2 -> x3, blocking collectives: 30.9 us -> 62.9 us  [exchange(): return lax.all_to_all(x, axes, split_axis=0, concat_axis=0, tiled=True)]
    all_to_all x1 -> x0, waiting for transfers between devices: 18.1 us -> none  [exchange(): return lax.all_to_all(x, axes, split_axis=0, concat_axis=0, tiled=True)]
    all_to_all x1 -> x0, starting transfers between devices: 3.7 us -> none  [exchange(): return lax.all_to_all(x, axes, split_axis=0, concat_axis=0, tiled=True)]
    ppermute x4, waiting for transfers between devices: 4.82 us -> 1.31 us  [across(): return lax.ppermute(x, 'core', SWAP)]
    ppermute x4, starting transfers between devices: 28.6 us -> 25.2 us  [across(): return lax.ppermute(x, 'core', SWAP)]
    unnamed x26 -> x24, local copies, waits for them, and re-layouts: 5.08 us -> 5.18 us
  transfers between devices with their start and end apart: 12 -> 11, of which waited for: 8 -> 5; matrix products, arithmetic and copies ran while one was open for 0% -> 0% of each run, Pallas kernels for 7% -> 7%
where the time goes in v2:
time: 158 us; the launch traced here: 157 us
  blocking collectives  62.9 us (40%)
  starting transfers between devices  44.4 us (28%)
  waiting for transfers between devices  26.3 us (17%)
  Pallas kernels  18 us (11%)
  local copies, waits for them, and re-layouts  5.18 us (3%)
    all_to_all x3, blocking collectives, exchange(): return lax.all_to_all(x, axes, split_axis=0, concat_axis=0, tiled=True)  62.9 us
    ppermute x4, starting transfers between devices, across(): return lax.ppermute(x, 'core', SWAP)  25.2 us
    ppermute x6, waiting for transfers between devices, hop(): lax.ppermute(x, 'y', [(i, (i + distance) % chips) for i in range(chips)])  19.2 us
    ppermute x6, starting transfers between devices, hop(): lax.ppermute(x, 'y', [(i, (i + distance) % chips) for i in range(chips)])  16.9 us
    pallas_call x4, Pallas kernels, gate_up(): pl.pallas_call(functools.partial(gate_up_kernel, tuple((len(blocks) for b...  12.4 us
    ppermute x1, waiting for transfers between devices, local(): lax.ppermute(jnp.where(core[0] == 0, up_y, down_y), ('y', 'core'), pairs)  5.79 us
    unnamed x24, local copies, waits for them, and re-layouts  5.18 us
    pallas_call x1, Pallas kernels, down(): pl.pallas_call(down_kernel, grid=(2,), out_shape=jax.ShapeDtypeStruct((no...  3.53 us
  transfers between devices with their start and end apart: 11, of which 5 were waited for; matrix products, arithmetic and copies ran while one was open for 0% of the time, Pallas kernels for 7%

profile of v2, /device:TPU:1, one launch (start us, length us, event | category | flops | bytes accessed | tf_op | source)
XLA Modules:
  0.0 157.1 jit_solution(14268330758856574742)
XLA Ops:
  0.0 16.1 %collective-permute-start = (bf16[448,256]{1,0:T(8,128)(2,1)}, bf16[448,256]{1,0:T(8,128)(2,1)S(1)}, u32[]{:S(2)}, u32[]{:S(2)}) collective-permute-start(bf16[448,256]{1,0:T(8,128)(2,1)} %bitcast.36), channel_id=1, source_target_pairs={{0,1},{1,0},{2,3},{3,2},{4,5},{5,4},{6,7},{7,6},{8,9},{9,8},{10,11... | collective-permute-start | bytes 688136 | tf_op jit(solution)/shard_map/ppermute | solution.py:214
  16.1 1.3 collective-permute-done.other_ref
  17.4 0.0 copy-start.7
  17.4 0.9 copy-done.7
  18.3 0.0 copy-start.8
  18.3 0.7 copy-done.8
  19.0 0.8 shard_map.64
  19.7 0.0 copy-start.10
  19.7 2.3 %collective-permute-start.6 = (bf16[7168,128]{1,0:T(8,128)(2,1)}, bf16[7168,128]{1,0:T(8,128)(2,1)S(1)}, u32[]{:S(2)}, u32[]{:S(2)}) collective-permute-start(bf16[7168,128]{1,0:T(8,128)(2,1)} %bitcast.13), channel_id=1, source_target_pairs={{0,1},{1,0},{2,3},{3,2},{4,5},{5,4},{6,7},{7,6},{8,9},{9,8},{10,11... | collective-permute-start | bytes 5505032 | tf_op jit(solution)/shard_map/ppermute | solution.py:214
  22.0 2.0 %collective-permute-start.7 = (bf16[7168,128]{1,0:T(8,128)(2,1)}, bf16[7168,128]{1,0:T(8,128)(2,1)}, u32[]{:S(2)}, u32[]{:S(2)}) collective-permute-start(bf16[7168,128]{1,0:T(8,128)(2,1)} %bitcast.22), channel_id=1, source_target_pairs={{0,1},{1,0},{2,3},{3,2},{4,5},{5,4},{6,7},{7,6},{8,9},{9,8},{10,11... | collective-permute-start | bytes 5505032 | tf_op jit(solution)/shard_map/ppermute | solution.py:214
  24.1 11.8 %all_to_all.15 = bf16[4,80,896]{2,1,0:T(8,128)(2,1)S(1)} all-to-all(bf16[4,80,896]{2,1,0:T(8,128)(2,1)S(1)} %get-tuple-element.17), channel_id=1, replica_groups=mesh['dp'=16,'node'=4,'y'=8,'core'=2] {'node'}, dimensions={0} | all-to-all | bytes 1146880 | tf_op jit(solution)/shard_map/all_to_all | solution.py:217
  35.9 0.0 copy-done.10
  35.9 1.9 %collective-permute-start.4 = (bf16[320,896]{1,0:T(8,128)(2,1)S(1)}, bf16[320,896]{1,0:T(8,128)(2,1)}, u32[]{:S(2)}, u32[]{:S(2)}) collective-permute-start(bf16[320,896]{1,0:T(8,128)(2,1)S(1)} %bitcast.32), channel_id=1, source_target_pairs={{0,14},{2,0},{4,2},{6,4},{8,6},{10,8},{12,10},{14,12},{1,15},{3,1}... | collective-permute-start | bytes 1720328 | tf_op jit(solution)/shard_map/ppermute | solution.py:211
  37.9 3.4 %collective-permute-start.1 = (bf16[320,896]{1,0:T(8,128)(2,1)S(1)}, bf16[320,896]{1,0:T(8,128)(2,1)}, u32[]{:S(2)}, u32[]{:S(2)}) collective-permute-start(bf16[320,896]{1,0:T(8,128)(2,1)S(1)} %bitcast.33), channel_id=1, source_target_pairs={{0,2},{2,4},{4,6},{6,8},{8,10},{10,12},{12,14},{14,0},{1,3},{3,5},... | collective-permute-start | bytes 1720328 | tf_op jit(solution)/shard_map/ppermute | solution.py:211
  41.2 9.7 %collective-permute-done.4.refs_2_ = bf16[320,896]{1,0:T(8,128)(2,1)} collective-permute-done((bf16[320,896]{1,0:T(8,128)(2,1)S(1)}, bf16[320,896]{1,0:T(8,128)(2,1)}, u32[]{:S(2)}, u32[]{:S(2)}) %collective-permute-start.4) | collective-permute-done | bytes 573472 | tf_op jit(solution)/shard_map/ppermute | solution.py:211
  50.9 3.4 %collective-permute-start.5 = (bf16[320,896]{1,0:T(8,128)(2,1)}, bf16[320,896]{1,0:T(8,128)(2,1)S(1)}, u32[]{:S(2)}, u32[]{:S(2)}) collective-permute-start(bf16[320,896]{1,0:T(8,128)(2,1)} %collective-permute-done.4.refs_2_), channel_id=1, source_target_pairs={{0,14},{2,0},{4,2},{6,4},{8,6},{10,8},{12,10},{14,12},{1,15},{3,1}... | collective-permute-start | bytes 1720328 | tf_op jit(solution)/shard_map/ppermute | solution.py:211
  54.3 0.0 collective-permute-done.1.refs_1_
  54.3 1.9 %collective-permute-start.2 = (bf16[320,896]{1,0:T(8,128)(2,1)}, bf16[320,896]{1,0:T(8,128)(2,1)S(1)}, u32[]{:S(2)}, u32[]{:S(2)}) collective-permute-start(bf16[320,896]{1,0:T(8,128)(2,1)} %collective-permute-done.1.refs_1_), channel_id=1, source_target_pairs={{0,2},{2,4},{4,6},{6,8},{8,10},{10,12},{12,14},{14,0},{1,3},{3,5},... | collective-permute-start | bytes 1720328 | tf_op jit(solution)/shard_map/ppermute | solution.py:211
  56.3 0.1 pad_add_fusion.idx_ref
  56.3 0.0 collective-permute-done.6.refs_5_.refs_9_.refs_13_.refs_4_.refs_8_.refs_3_
  56.3 0.0 copy-start.2
  56.3 0.0 collective-permute-done.7.refs_6_.refs_10_.refs_14_.refs_5_.refs_9_.refs_4_
  56.3 1.2 copy-done.2
  57.6 4.5 %shard_map.65.refs_10_ = f32[320,512]{1,0:T(8,128)} custom-call(s32[9]{0:T(128)S(1)} %pad_add_fusion.idx_ref, bf16[320,896]{1,0:T(8,128)(2,1)S(1)} %bitcast.34, bf16[320,896]{1,0:T(8,128)(2,1)} %collective-permute-done.1.refs_1_, bf16[320,896]{1,0:T(8,128)(2,1)} %collective-permute-done.4.refs_2_, bf16[7168,128]{1,0:T(8,128)(2,1)} %bitcast.14, ...), custom_call_target="tpu_custom_call" | custom-call | flops 880803840 | bytes 5128192 | tf_op jit(solution)/shard_map/pallas_call | solution.py:113
  62.1 0.0 copy-start.5
  62.1 0.6 copy-done.5
  62.7 4.8 %collective-permute-start.10 = (bf16[448,2048]{1,0:T(8,128)(2,1)}, bf16[448,2048]{1,0:T(8,128)(2,1)}, u32[]{:S(2)}, u32[]{:S(2)}) collective-permute-start(bf16[448,2048]{1,0:T(8,128)(2,1)} %bitcast.7.own_ref), channel_id=1, source_target_pairs={{0,1},{1,0},{2,3},{3,2},{4,5},{5,4},{6,7},{7,6},{8,9},{9,8},{10,11... | collective-permute-start | bytes 5505032 | tf_op jit(solution)/shard_map/ppermute | solution.py:214
  67.5 0.0 collective-permute-done.5.refs_1_
  67.5 4.3 %collective-permute-start.8 = (bf16[320,896]{1,0:T(8,128)(2,1)S(1)}, bf16[320,896]{1,0:T(8,128)(2,1)S(1)}, u32[]{:S(2)}, u32[]{:S(2)}) collective-permute-start(bf16[320,896]{1,0:T(8,128)(2,1)S(1)} %collective-permute-done.5.refs_1_), channel_id=1, source_target_pairs={{0,14},{2,0},{4,2},{6,4},{8,6},{10,8},{12,10},{14,12},{1,15},{3,1}... | collective-permute-start | bytes 1720328 | tf_op jit(solution)/shard_map/ppermute | solution.py:211
  71.9 0.0 collective-permute-done.2.refs_0_
  71.9 1.9 %collective-permute-start.3 = (bf16[320,896]{1,0:T(8,128)(2,1)S(1)}, bf16[320,896]{1,0:T(8,128)(2,1)S(1)}, u32[]{:S(2)}, u32[]{:S(2)}) collective-permute-start(bf16[320,896]{1,0:T(8,128)(2,1)S(1)} %collective-permute-done.2.refs_0_), channel_id=1, source_target_pairs={{0,2},{2,4},{4,6},{6,8},{8,10},{10,12},{12,14},{14,0},{1,3},{3,5},... | collective-permute-start | bytes 1720328 | tf_op jit(solution)/shard_map/ppermute | solution.py:211
  73.8 0.0 copy-start.4
  73.8 1.1 copy-done.4
  74.9 0.0 copy-start.6
  74.9 0.7 copy-done.6
  75.5 2.9 %shard_map.66.refs_10_ = f32[320,512]{1,0:T(8,128)S(1)} custom-call(s32[9]{0:T(128)S(1)} %copy-done.6, bf16[320,896]{1,0:T(8,128)(2,1)S(1)} %collective-permute-done.2.refs_0_, bf16[320,896]{1,0:T(8,128)(2,1)S(1)} %collective-permute-done.5.refs_1_, bf16[7168,128]{1,0:T(8,128)(2,1)} %bitcast.17, ...), custom_call_target="tpu_custom_call", output_to_operand_aliasing={{}: (11, {})} | custom-call | flops 587202560 | bytes 3637248 | tf_op jit(solution)/shard_map/pallas_call | solution.py:113
  78.4 4.6 %collective-permute-done.8.refs_1_ = bf16[320,896]{1,0:T(8,128)(2,1)S(1)} collective-permute-done((bf16[320,896]{1,0:T(8,128)(2,1)S(1)}, bf16[320,896]{1,0:T(8,128)(2,1)S(1)}, u32[]{:S(2)}, u32[]{:S(2)}) %collective-permute-start.8) | collective-permute-done | bytes 573472 | tf_op jit(solution)/shard_map/ppermute | solution.py:211
  83.0 5.0 %collective-permute-done.3.refs_0_ = bf16[320,896]{1,0:T(8,128)(2,1)S(1)} collective-permute-done((bf16[320,896]{1,0:T(8,128)(2,1)S(1)}, bf16[320,896]{1,0:T(8,128)(2,1)S(1)}, u32[]{:S(2)}, u32[]{:S(2)}) %collective-permute-start.3) | collective-permute-done | bytes 573472 | tf_op jit(solution)/shard_map/ppermute | solution.py:211
  88.0 0.1 broadcast_select_fusion
  88.1 0.0 copy-start
  88.1 0.0 copy-start.1
  88.1 0.0 copy-start.3
  88.1 2.3 %collective-permute-start.9 = (bf16[320,896]{1,0:T(8,128)(2,1)S(1)}, bf16[320,896]{1,0:T(8,128)(2,1)S(1)}, u32[]{:S(2)}, u32[]{:S(2)}) collective-permute-start(bf16[320,896]{1,0:T(8,128)(2,1)S(1)} %broadcast_select_fusion), channel_id=1, source_target_pairs={{0,2},{1,15},{2,4},{3,1},{4,6},{5,3},{6,8},{7,5},{8,10},{9,7},{10,... | collective-permute-start | bytes 1720328 | tf_op jit(solution)/shard_map/ppermute | solution.py:238
  90.4 2.9 %shard_map.67.refs_5_ = f32[320,512]{1,0:T(8,128)S(1)} custom-call(s32[9]{0:T(128)S(1)} %copy-done.6, bf16[320,896]{1,0:T(8,128)(2,1)S(1)} %collective-permute-done.3.refs_0_, bf16[320,896]{1,0:T(8,128)(2,1)S(1)} %collective-permute-done.8.refs_1_, bf16[7168,128]{1,0:T(8,128)(2,1)} %bitcast.19, ...), custom_call_target="tpu_custom_call", output_to_operand_aliasing={{}: (11, {})} | custom-call | flops 587202560 | bytes 3637248 | tf_op jit(solution)/shard_map/pallas_call | solution.py:113
  93.3 0.0 collective-permute-done.10.other_ref
  93.3 5.8 %collective-permute-done.9.refs_0_ = bf16[320,896]{1,0:T(8,128)(2,1)S(1)} collective-permute-done((bf16[320,896]{1,0:T(8,128)(2,1)S(1)}, bf16[320,896]{1,0:T(8,128)(2,1)S(1)}, u32[]{:S(2)}, u32[]{:S(2)}) %collective-permute-start.9) | collective-permute-done | bytes 573472 | tf_op jit(solution)/shard_map/ppermute | solution.py:238
  99.1 0.0 copy-done
  99.1 0.0 copy-done.1
  99.1 0.0 copy-done.3
  99.1 2.1 %shard_map.68 = bf16[8,320,256]{2,1,0:T(8,128)(2,1)S(1)} custom-call(s32[9]{0:T(128)S(1)} %copy-done.6, bf16[320,896]{1,0:T(8,128)(2,1)S(1)} %collective-permute-done.9.refs_0_, bf16[7168,128]{1,0:T(8,128)(2,1)S(1)} %bitcast.21, bf16[7168,128]{1,0:T(8,128)(2,1)S(1)} %bitcast.30, bf16[7168,128]{1,0:T(8,128)(2,1)S(1)} %copy-done.3, ...), custom_call_target="tpu_custom_call" | custom-call | flops 293601280 | bytes 2146304 | tf_op jit(solution)/shard_map/pallas_call | solution.py:113
  101.2 31.7 %all_to_all.16.hidden_ref = bf16[8,320,256]{2,1,0:T(8,128)(2,1)S(1)} all-to-all(bf16[8,320,256]{2,1,0:T(8,128)(2,1)S(1)} %shard_map.68), channel_id=1, replica_groups=mesh['dp'=16,'node'=4,'y'=8,'core'=2] {'y'}, dimensions={0} | all-to-all | bytes 2621440 | tf_op jit(solution)/shard_map/all_to_all | solution.py:217
  132.9 0.0 copy-start.9
  132.9 0.0 copy-start.11
  132.9 3.5 %shard_map.69 = bf16[4,2,80,448]{3,2,1,0:T(8,128)(2,1)S(1)} custom-call(s32[1]{0:T(128)} %bitcast.core_ref, bf16[8,320,256]{2,1,0:T(8,128)(2,1)S(1)} %all_to_all.16.hidden_ref, bf16[448,2048]{1,0:T(8,128)(2,1)} %bitcast.7.own_ref, bf16[448,2048]{1,0:T(8,128)(2,1)} %collective-permute-done.10.other_ref), custom_call_target="tpu_custom_call" | custom-call | flops 1174405120 | bytes 6000000 | tf_op jit(solution)/shard_map/pallas_call | solution.py:156
  136.5 19.4 %all_to_all.17 = bf16[8,80,448]{2,1,0:T(8,128)(2,1)S(1)} all-to-all(bf16[8,80,448]{2,1,0:T(8,128)(2,1)S(1)} %bitcast.31), channel_id=1, replica_groups=mesh['dp'=16,'node'=4,'y'=8,'core'=2] {'node','core'}, dimensions={0} | all-to-all | bytes 1146880 | tf_op jit(solution)/shard_map/all_to_all | solution.py:217
  155.8 0.0 copy-done.9
  155.8 0.0 copy-done.11
  155.8 1.3 shard_map.70
  (1 shorter events, 0.0 us)
Async XLA Ops:
  0.0 17.4 %collective-permute-start = (bf16[448,256]{1,0:T(8,128)(2,1)}, bf16[448,256]{1,0:T(8,128)(2,1)S(1)}, u32[]{:S(2)}, u32[]{:S(2)}) collective-permute-start(bf16[448,256]{1,0:T(8,128)(2,1)} %bitcast.36), channel_id=1, source_target_pairs={{0,1},{1,0},{2,3},{3,2},{4,5},{5,4},{6,7},{7,6},{8,9},{9,8},{10,11... | collective-permute-start | bytes 688136 | tf_op jit(solution)/shard_map/ppermute | solution.py:214
  17.4 0.9 copy-start.7
  18.3 0.7 copy-start.8
  19.7 16.2 %copy-start.10 = (s32[2,256]{1,0:T(2,128)}, s32[2,256]{1,0:T(2,128)S(1)}, u32[]{:S(2)}) copy-start(s32[2,256]{1,0:T(2,128)S(1)} %get-tuple-element.26.pick_ref) | copy-start | bytes 6148
  19.7 36.6 %collective-permute-start.6 = (bf16[7168,128]{1,0:T(8,128)(2,1)}, bf16[7168,128]{1,0:T(8,128)(2,1)S(1)}, u32[]{:S(2)}, u32[]{:S(2)}) collective-permute-start(bf16[7168,128]{1,0:T(8,128)(2,1)} %bitcast.13), channel_id=1, source_target_pairs={{0,1},{1,0},{2,3},{3,2},{4,5},{5,4},{6,7},{7,6},{8,9},{9,8},{10,11... | collective-permute-start | bytes 5505032 | tf_op jit(solution)/shard_map/ppermute | solution.py:214
  22.0 34.3 %collective-permute-start.7 = (bf16[7168,128]{1,0:T(8,128)(2,1)}, bf16[7168,128]{1,0:T(8,128)(2,1)}, u32[]{:S(2)}, u32[]{:S(2)}) collective-permute-start(bf16[7168,128]{1,0:T(8,128)(2,1)} %bitcast.22), channel_id=1, source_target_pairs={{0,1},{1,0},{2,3},{3,2},{4,5},{5,4},{6,7},{7,6},{8,9},{9,8},{10,11... | collective-permute-start | bytes 5505032 | tf_op jit(solution)/shard_map/ppermute | solution.py:214
  35.9 15.0 %collective-permute-start.4 = (bf16[320,896]{1,0:T(8,128)(2,1)S(1)}, bf16[320,896]{1,0:T(8,128)(2,1)}, u32[]{:S(2)}, u32[]{:S(2)}) collective-permute-start(bf16[320,896]{1,0:T(8,128)(2,1)S(1)} %bitcast.32), channel_id=1, source_target_pairs={{0,14},{2,0},{4,2},{6,4},{8,6},{10,8},{12,10},{14,12},{1,15},{3,1}... | collective-permute-start | bytes 1720328 | tf_op jit(solution)/shard_map/ppermute | solution.py:211
  37.9 16.5 %collective-permute-start.1 = (bf16[320,896]{1,0:T(8,128)(2,1)S(1)}, bf16[320,896]{1,0:T(8,128)(2,1)}, u32[]{:S(2)}, u32[]{:S(2)}) collective-permute-start(bf16[320,896]{1,0:T(8,128)(2,1)S(1)} %bitcast.33), channel_id=1, source_target_pairs={{0,2},{2,4},{4,6},{6,8},{8,10},{10,12},{12,14},{14,0},{1,3},{3,5},... | collective-permute-start | bytes 1720328 | tf_op jit(solution)/shard_map/ppermute | solution.py:211
  50.9 16.6 %collective-permute-start.5 = (bf16[320,896]{1,0:T(8,128)(2,1)}, bf16[320,896]{1,0:T(8,128)(2,1)S(1)}, u32[]{:S(2)}, u32[]{:S(2)}) collective-permute-start(bf16[320,896]{1,0:T(8,128)(2,1)} %collective-permute-done.4.refs_2_), channel_id=1, source_target_pairs={{0,14},{2,0},{4,2},{6,4},{8,6},{10,8},{12,10},{14,12},{1,15},{3,1}... | collective-permute-start | bytes 1720328 | tf_op jit(solution)/shard_map/ppermute | solution.py:211
  54.3 17.5 %collective-permute-start.2 = (bf16[320,896]{1,0:T(8,128)(2,1)}, bf16[320,896]{1,0:T(8,128)(2,1)S(1)}, u32[]{:S(2)}, u32[]{:S(2)}) collective-permute-start(bf16[320,896]{1,0:T(8,128)(2,1)} %collective-permute-done.1.refs_1_), channel_id=1, source_target_pairs={{0,2},{2,4},{4,6},{6,8},{8,10},{10,12},{12,14},{14,0},{1,3},{3,5},... | collective-permute-start | bytes 1720328 | tf_op jit(solution)/shard_map/ppermute | solution.py:211
  56.3 1.2 copy-start.2
  62.1 0.6 copy-start.5
  62.7 30.7 %collective-permute-start.10 = (bf16[448,2048]{1,0:T(8,128)(2,1)}, bf16[448,2048]{1,0:T(8,128)(2,1)}, u32[]{:S(2)}, u32[]{:S(2)}) collective-permute-start(bf16[448,2048]{1,0:T(8,128)(2,1)} %bitcast.7.own_ref), channel_id=1, source_target_pairs={{0,1},{1,0},{2,3},{3,2},{4,5},{5,4},{6,7},{7,6},{8,9},{9,8},{10,11... | collective-permute-start | bytes 5505032 | tf_op jit(solution)/shard_map/ppermute | solution.py:214
  67.5 15.5 %collective-permute-start.8 = (bf16[320,896]{1,0:T(8,128)(2,1)S(1)}, bf16[320,896]{1,0:T(8,128)(2,1)S(1)}, u32[]{:S(2)}, u32[]{:S(2)}) collective-permute-start(bf16[320,896]{1,0:T(8,128)(2,1)S(1)} %collective-permute-done.5.refs_1_), channel_id=1, source_target_pairs={{0,14},{2,0},{4,2},{6,4},{8,6},{10,8},{12,10},{14,12},{1,15},{3,1}... | collective-permute-start | bytes 1720328 | tf_op jit(solution)/shard_map/ppermute | solution.py:211
  71.9 16.1 %collective-permute-start.3 = (bf16[320,896]{1,0:T(8,128)(2,1)S(1)}, bf16[320,896]{1,0:T(8,128)(2,1)S(1)}, u32[]{:S(2)}, u32[]{:S(2)}) collective-permute-start(bf16[320,896]{1,0:T(8,128)(2,1)S(1)} %collective-permute-done.2.refs_0_), channel_id=1, source_target_pairs={{0,2},{2,4},{4,6},{6,8},{8,10},{10,12},{12,14},{14,0},{1,3},{3,5},... | collective-permute-start | bytes 1720328 | tf_op jit(solution)/shard_map/ppermute | solution.py:211
  73.8 1.1 copy-start.4
  74.9 0.7 copy-start.6
  88.1 11.0 %copy-start = (bf16[1,7168,128]{2,1,0:T(8,128)(2,1)S(1)}, bf16[1,7168,128]{2,1,0:T(8,128)(2,1)}, u32[]{:S(2)}) copy-start(bf16[1,7168,128]{2,1,0:T(8,128)(2,1)} %param.9) | copy-start | bytes 5505028
  88.1 11.0 %copy-start.1 = (bf16[1,7168,128]{2,1,0:T(8,128)(2,1)S(1)}, bf16[1,7168,128]{2,1,0:T(8,128)(2,1)}, u32[]{:S(2)}) copy-start(bf16[1,7168,128]{2,1,0:T(8,128)(2,1)} %param.10) | copy-start | bytes 5505028
  88.1 11.0 %copy-start.3 = (bf16[7168,128]{1,0:T(8,128)(2,1)S(1)}, bf16[7168,128]{1,0:T(8,128)(2,1)}, u32[]{:S(2)}) copy-start(bf16[7168,128]{1,0:T(8,128)(2,1)} %copy-done.2) | copy-start | bytes 5505028
  88.1 11.0 %collective-permute-start.9 = (bf16[320,896]{1,0:T(8,128)(2,1)S(1)}, bf16[320,896]{1,0:T(8,128)(2,1)S(1)}, u32[]{:S(2)}, u32[]{:S(2)}) collective-permute-start(bf16[320,896]{1,0:T(8,128)(2,1)S(1)} %broadcast_select_fusion), channel_id=1, source_target_pairs={{0,2},{1,15},{2,4},{3,1},{4,6},{5,3},{6,8},{7,5},{8,10},{9,7},{10,... | collective-permute-start | bytes 1720328 | tf_op jit(solution)/shard_map/ppermute | solution.py:238
  132.9 22.9 %copy-start.9 = (f32[256,2]{0,1:T(2,128)S(1)}, f32[256,2]{0,1:T(2,128)}, u32[]{:S(2)}) copy-start(f32[256,2]{0,1:T(2,128)} %param.8) | copy-start | bytes 6148
  132.9 22.9 %copy-start.11 = (s32[2,256]{1,0:T(2,128)S(1)}, s32[2,256]{1,0:T(2,128)}, u32[]{:S(2)}) copy-start(s32[2,256]{1,0:T(2,128)} %copy-done.10) | copy-start | bytes 6148
